TPU v7x, 1024 devices: a whole 4x4x32 slice. The times are simulated.
1024 devices in a mesh: dp: 64 (over z, core), expert: 16 (over x, y).
Axes of the slice: x: 4, y: 4, z: 32, core: 2. Of those that a mesh axis runs over, the one named last changes fastest.
Arguments:
- tokens: bfloat16 [16384, 2048], P(('dp', 'expert')), may hold values from -6 to 6
- grad_out: bfloat16 [16384, 2048], P(('dp', 'expert')), may hold values from -6 to 6
- gate_probs: bfloat16 [16384, 8], P(('dp', 'expert')), may hold values from 0.049804688 to 1
- routes: int32 [16384, 8], P(('dp', 'expert')), may hold values from 0 to 15, as said below
- capacity: int32 [64, 16], P('dp', 'expert'), may hold values from 64 to 128, as said below
- pair_mask: int32 [16], P('expert'), may hold values from 1 to 32, as said below
- gate_up_weight: bfloat16 [16, 2048, 1536], P('expert'), may hold values from -0.125 to 0.125
- down_weight: bfloat16 [16, 2048, 768], P('expert'), may hold values from -0.21875 to 0.21875
Outputs:
- layer_out: bfloat16 [16384, 2048], P(('dp', 'expert'))
- input_grad: bfloat16 [16384, 2048], P(('dp', 'expert'))
- gate_grad: float32 [16384, 8], P(('dp', 'expert'))
Inputs may be any that keep to these rules, and one draw needn't show every extreme that they name: `routes`: each token names 8 different experts. The tokens of one device name any one expert at most 12 times; one expert, the same for all devices, is named exactly 12 times by the tokens of every device. `capacity`: both ends of the range occur in every draw. `pair_mask`: each entry is a power of two; both ends of the range occur in every draw.
All inputs are finite; a program needn't handle non-finite values.
Results may differ from a plain program's by a relative error of at most 0.01.
Values may be sent and summed in bfloat16 or wider, within the bound.
A program may use at most 64 MiB of HBM per device.

v0:
```python
import jax
import jax.numpy as jnp
from jax import lax
from jax.sharding import PartitionSpec as P

TOPK = 8
EXPERTS = 16
OVF = 16


far_position = 1 << 20


def swapped(shard, axis, apart):
    return lax.ppermute(shard, axis, [(i, i ^ 1 << apart) for i in range(lax.axis_size(axis))])


def pick_rows(table, index):
    return jnp.take(table, index, axis=0, mode="fill", fill_value=0)


def expert_rows(row_input, row_scaled, w_gate_up, w_down):
    hidden_units = w_down.shape[1]
    both = jnp.dot(row_input, w_gate_up, preferred_element_type=jnp.float32)
    gate_pre = both[:, :hidden_units]
    up_pre = both[:, hidden_units:]
    sigma = jax.nn.sigmoid(gate_pre)
    swish = gate_pre * sigma
    hidden = (swish * up_pre).astype(jnp.bfloat16)
    outputs = lax.dot_general(
        hidden, w_down, (((1,), (1,)), ((), ())), preferred_element_type=jnp.float32
    ).astype(jnp.bfloat16)
    back_hidden = jnp.dot(row_scaled, w_down, preferred_element_type=jnp.float32)
    d_gate = back_hidden * up_pre * sigma * (1.0 + gate_pre * (1.0 - sigma))
    d_up = back_hidden * swish
    d_both = jnp.concatenate([d_gate, d_up], axis=1).astype(jnp.bfloat16)
    row_grads = lax.dot_general(
        d_both, w_gate_up, (((1,), (1,)), ((), ())), preferred_element_type=jnp.float32
    ).astype(jnp.bfloat16)
    return (outputs, row_grads)


def run_experts(row_input, row_scaled, gate_up_weight, down_weight):
    out_rows, grad_rows = expert_rows(row_input, row_scaled, gate_up_weight[0], down_weight[0])
    return (out_rows, grad_rows)


def serve_rows(
    pool_tokens,
    pool_scaled,
    queue_pos,
    item_local,
    queue_length,
    local_caps,
    pair_mask,
    gate_up_weight,
    down_weight,
    cap_rows,
):
    local_count = queue_length.shape[0]
    pool_size = pool_tokens.shape[0]
    pool_ids = jnp.arange(pool_size, dtype=jnp.int32)
    home_rows = jnp.minimum(queue_length, local_caps)
    spare_rows = local_caps - home_rows
    accepted = jnp.minimum(spare_rows, OVF)
    cap_item = local_caps[item_local]
    offset = queue_pos - cap_item
    spilled = (offset >= 0) & (offset < OVF)
    spill_slot = jnp.where(spilled, item_local * OVF + offset, local_count * OVF)
    spill_from = (
        jnp.full((local_count * OVF + 1,), pool_size, jnp.int32)
        .at[spill_slot]
        .set(pool_ids)[: local_count * OVF]
    )
    outgoing = jnp.stack([pick_rows(pool_tokens, spill_from), pick_rows(pool_scaled, spill_from)])
    home_slot = jnp.where(
        queue_pos < cap_item, item_local * cap_rows + queue_pos, local_count * cap_rows
    )
    home_from = (
        jnp.full((local_count * cap_rows + 1,), pool_size, jnp.int32)
        .at[home_slot]
        .set(pool_ids)[: local_count * cap_rows]
    )
    home_tokens = pick_rows(pool_tokens, home_from)
    home_scaled = pick_rows(pool_scaled, home_from)
    slot_ids = jnp.arange(local_count * OVF, dtype=jnp.int32)
    slot_local = slot_ids // OVF
    slot_index = slot_ids % OVF
    slot_mask = pair_mask[slot_local]
    is_live = slot_index < accepted[slot_local]
    levels = lax.axis_size("dp").bit_length() - 1
    incoming = jnp.zeros_like(outgoing)
    for bit_index in range(levels):
        received = swapped(outgoing, "dp", bit_index)
        incoming = jnp.where((slot_mask == 1 << bit_index)[None, :, None], received, incoming)
    incoming = jnp.where(is_live[None, :, None], incoming, jnp.zeros_like(incoming))
    in_slot = jnp.where(
        is_live, slot_local * cap_rows + home_rows[slot_local] + slot_index, local_count * cap_rows
    )
    in_from = (
        jnp.full((local_count * cap_rows + 1,), local_count * OVF, jnp.int32)
        .at[in_slot]
        .set(slot_ids)[: local_count * cap_rows]
    )
    joined_tokens = home_tokens + pick_rows(incoming[0], in_from)
    joined_scaled = home_scaled + pick_rows(incoming[1], in_from)
    home_out, home_grad = run_experts(joined_tokens, joined_scaled, gate_up_weight, down_weight)
    returning = jnp.stack([pick_rows(home_out, in_slot), pick_rows(home_grad, in_slot)])
    answered = jnp.zeros_like(returning)
    for bit_index in range(levels):
        received_back = swapped(returning, "dp", bit_index)
        answered = jnp.where((slot_mask == 1 << bit_index)[None, :, None], received_back, answered)
    pool_out = pick_rows(home_out, home_slot) + pick_rows(answered[0], spill_slot)
    pool_grad = pick_rows(home_grad, home_slot) + pick_rows(answered[1], spill_slot)
    return (pool_out, pool_grad)


def body(tokens, grad_out, gate_probs, routes, capacity, pair_mask, gate_up_weight, down_weight):
    tok_count = tokens.shape[0]
    model_width = tokens.shape[1]
    local_count = gate_up_weight.shape[0]
    group_size = lax.axis_size("expert")
    member = lax.axis_index("expert")
    cap_rows = group_size * tok_count * TOPK // EXPERTS
    local_caps = capacity[0]
    all_tokens, all_grad, all_gates, all_routes = (
        lax.all_gather(tokens, "expert", axis=0, tiled=True),
        lax.all_gather(grad_out, "expert", axis=0, tiled=True),
        lax.all_gather(gate_probs, "expert", axis=0, tiled=True),
        lax.all_gather(routes.astype(jnp.bfloat16), "expert", axis=0, tiled=True),
    )
    row_tokens = all_tokens.shape[0]
    row_routes = row_tokens * TOPK
    span = cap_rows + OVF
    flat_routes = all_routes.astype(jnp.int32).reshape(row_routes)
    local_ids = member * local_count + jnp.arange(local_count, dtype=jnp.int32)
    route_match = (flat_routes[:, None] == local_ids[None, :]).astype(jnp.int32)
    queue_all = jnp.cumsum(route_match, axis=0) - 1
    queue_length = jnp.sum(route_match, axis=0)
    pool_slot = jnp.where(
        (route_match == 1) & (queue_all < span),
        jnp.arange(local_count, dtype=jnp.int32)[None, :] * span + queue_all,
        local_count * span,
    )
    route_ids = jnp.arange(row_routes, dtype=jnp.int32)[:, None]
    pool_route = (
        jnp.full((local_count * span + 1,), row_routes, jnp.int32)
        .at[pool_slot.reshape(-1)]
        .set(route_ids.reshape(-1))[: local_count * span]
    )
    item_index = jnp.arange(local_count * span, dtype=jnp.int32)
    item_local = item_index // span
    item_queue = item_index % span
    queue_pos = jnp.where(item_queue < queue_length[item_local], item_queue, far_position)
    pool_token = pool_route // TOPK
    pool_gate = jnp.take(
        all_gates.reshape(row_routes), pool_route, mode="fill", fill_value=0
    ).astype(jnp.float32)
    pool_grad_in = pick_rows(all_grad, pool_token)
    pool_scaled = (pool_gate[:, None] * pool_grad_in.astype(jnp.float32)).astype(jnp.bfloat16)
    pool_tokens = pick_rows(all_tokens, pool_token)
    pool_out, pool_grad = serve_rows(
        pool_tokens,
        pool_scaled,
        queue_pos,
        item_local,
        queue_length,
        local_caps,
        pair_mask,
        gate_up_weight,
        down_weight,
        cap_rows,
    )
    out_float = pool_out.astype(jnp.float32)
    out_terms = (
        jnp.zeros((row_tokens, model_width), jnp.float32)
        .at[pool_token]
        .add(pool_gate[:, None] * out_float, mode="drop")
    )
    grad_terms = (
        jnp.zeros((row_tokens, model_width), jnp.float32)
        .at[pool_token]
        .add(pool_grad.astype(jnp.float32), mode="drop")
    )
    gate_terms = (
        jnp.zeros((row_routes,), jnp.float32)
        .at[pool_route]
        .add(jnp.sum(pool_grad_in.astype(jnp.float32) * out_float, axis=1), mode="drop")
        .reshape(row_tokens, TOPK)
    )
    summed_out, summed_grad, summed_gate = (
        lax.psum_scatter(out_terms, "expert", scatter_dimension=0, tiled=True),
        lax.psum_scatter(grad_terms, "expert", scatter_dimension=0, tiled=True),
        lax.psum_scatter(gate_terms, "expert", scatter_dimension=0, tiled=True),
    )
    return (summed_out.astype(jnp.bfloat16), summed_grad.astype(jnp.bfloat16), summed_gate)


def solution(mesh):
    return jax.shard_map(
        body,
        mesh=mesh,
        in_specs=(
            P(("dp", "expert"), None),
            P(("dp", "expert"), None),
            P(("dp", "expert"), None),
            P(("dp", "expert"), None),
            P("dp", "expert"),
            P("expert"),
            P("expert", None, None),
            P("expert", None, None),
        ),
        out_specs=(P(("dp", "expert"), None), P(("dp", "expert"), None), P(("dp", "expert"), None)),
        check_vma=False,
    )
```

profile of v0, /device:TPU:6, one launch (start us, length us, event | category | flops | bytes accessed | tf_op | source)
XLA Modules:
  0.0 597.0 jit_solution(1706415513742245332)
XLA Ops:
  9.4 33.4 %all-gather = bf16[16,16,8]{1,2,0:T(8,128)(2,1)S(1)} all-gather(bf16[1,16,8]{1,2,0:T(8,128)(2,1)S(1)} %convert_bitcast_fusion), channel_id=1, replica_groups=mesh['dp'=64,'expert'=16] {'expert'}, dimensions={0}, use_global_device_ids=true | all-gather | bytes 4352 | tf_op jit(solution)/shard_map/all_gather | solution.py:130
  45.3 8.0 %scatter_custom_fusion = s32[145]{0:T(256)S(1)} fusion(s32[2048]{0:T(1024)S(1)} %bitcast.70, s32[2048]{0:T(1024)S(1)} %iota.47, s32[]{:T(128)} %constant.145.clone.1), kind=kCustom, calls=%fused_computation.160 | custom fusion | bytes 584 | tf_op jit(solution)/shard_map/scatter | solution.py:149
  54.7 20.9 %all-gather.1 = bf16[16,16,8]{1,2,0:T(8,128)(2,1)S(1)} all-gather(bf16[1,16,8]{1,2,0:T(8,128)(2,1)} %bitcast.71), channel_id=1, replica_groups=mesh['dp'=64,'expert'=16] {'expert'}, dimensions={0}, use_global_device_ids=true | all-gather | bytes 4352 | tf_op jit(solution)/shard_map/all_gather | solution.py:129
  81.9 15.9 %all-gather.5.cloned.1.call-done = bf16[256,2048]{1,0:T(8,128)(2,1)} async-done(((bf16[16,2048]{1,0:T(8,128)(2,1)}), bf16[256,2048]{1,0:T(8,128)(2,1)}) %all-gather.5.cloned.1.call-update) | async-done | bytes 1048592 | tf_op jit(solution)/shard_map/all_gather | solution.py:127
  97.8 3.7 gather_fusion.1
  101.5 2.0 broadcast_select_fusion.1
  105.3 74.7 %all-gather.7.cloned.1.call-done = bf16[256,2048]{1,0:T(8,128)(2,1)} async-done(((bf16[16,2048]{1,0:T(8,128)(2,1)}), bf16[256,2048]{1,0:T(8,128)(2,1)}) %all-gather.7.cloned.1.call-update) | async-done | bytes 1048592 | tf_op jit(solution)/shard_map/all_gather | solution.py:128
  180.1 3.7 gather_fusion.4
  183.8 2.2 fusion.14
  190.4 3.4 collective-permute-start.4
  193.9 4.5 collective-permute-start.3
  198.3 7.6 %collective-permute-start.2 = (bf16[2,16,2048]{2,1,0:T(8,128)(2,1)S(1)}, bf16[2,16,2048]{2,1,0:T(8,128)(2,1)}, u32[]{:S(2)}, u32[]{:S(2)}) collective-permute-start(bf16[2,16,2048]{2,1,0:T(8,128)(2,1)S(1)} %pad_maximum_fusion), channel_id=1, source_target_pairs={{0,128},{16,144},{32,160},{48,176},{64,192},{80,208},{96,224},{112... | collective-permute-start | bytes 393224 | tf_op jit(solution)/shard_map/ppermute | solution.py:15
  206.0 12.8 %collective-permute-start.1 = (bf16[2,16,2048]{2,1,0:T(8,128)(2,1)S(1)}, bf16[2,16,2048]{2,1,0:T(8,128)(2,1)}, u32[]{:S(2)}, u32[]{:S(2)}) collective-permute-start(bf16[2,16,2048]{2,1,0:T(8,128)(2,1)S(1)} %pad_maximum_fusion), channel_id=1, source_target_pairs={{0,256},{16,272},{32,288},{48,304},{64,320},{80,336},{96,352},{112... | collective-permute-start | bytes 393224 | tf_op jit(solution)/shard_map/ppermute | solution.py:15
  218.8 6.2 %collective-permute-start = (bf16[2,16,2048]{2,1,0:T(8,128)(2,1)S(1)}, bf16[2,16,2048]{2,1,0:T(8,128)(2,1)}, u32[]{:S(2)}, u32[]{:S(2)}) collective-permute-start(bf16[2,16,2048]{2,1,0:T(8,128)(2,1)S(1)} %pad_maximum_fusion), channel_id=1, source_target_pairs={{0,512},{16,528},{32,544},{48,560},{64,576},{80,592},{96,608},{112... | collective-permute-start | bytes 393224 | tf_op jit(solution)/shard_map/ppermute | solution.py:15
  226.9 3.4 gather_fusion.2
  230.3 3.4 gather_fusion.9
  233.7 30.5 %collective-permute-done.1 = bf16[2,16,2048]{2,1,0:T(8,128)(2,1)} collective-permute-done((bf16[2,16,2048]{2,1,0:T(8,128)(2,1)S(1)}, bf16[2,16,2048]{2,1,0:T(8,128)(2,1)}, u32[]{:S(2)}, u32[]{:S(2)}) %collective-permute-start.1) | collective-permute-done | bytes 131104 | tf_op jit(solution)/shard_map/ppermute | solution.py:15
  268.6 4.2 fusion.2
  272.9 2.0 fusion.8
  278.3 5.9 fusion.11
  290.7 1.9 collective-permute-start.9
  292.6 10.4 %collective-permute-start.8 = (bf16[2,16,2048]{2,1,0:T(8,128)(2,1)S(1)}, bf16[2,16,2048]{2,1,0:T(8,128)(2,1)}, u32[]{:S(2)}, u32[]{:S(2)}) collective-permute-start(bf16[2,16,2048]{2,1,0:T(8,128)(2,1)S(1)} %pad_maximum_fusion.1), channel_id=1, source_target_pairs={{0,128},{16,144},{32,160},{48,176},{64,192},{80,208},{96,224},{112... | collective-permute-start | bytes 393224 | tf_op jit(solution)/shard_map/ppermute | solution.py:15
  303.0 7.1 %collective-permute-start.7 = (bf16[2,16,2048]{2,1,0:T(8,128)(2,1)S(1)}, bf16[2,16,2048]{2,1,0:T(8,128)(2,1)}, u32[]{:S(2)}, u32[]{:S(2)}) collective-permute-start(bf16[2,16,2048]{2,1,0:T(8,128)(2,1)S(1)} %pad_maximum_fusion.1), channel_id=1, source_target_pairs={{0,256},{16,272},{32,288},{48,304},{64,320},{80,336},{96,352},{112... | collective-permute-start | bytes 393224 | tf_op jit(solution)/shard_map/ppermute | solution.py:15
  310.1 10.7 %collective-permute-start.6 = (bf16[2,16,2048]{2,1,0:T(8,128)(2,1)S(1)}, bf16[2,16,2048]{2,1,0:T(8,128)(2,1)}, u32[]{:S(2)}, u32[]{:S(2)}) collective-permute-start(bf16[2,16,2048]{2,1,0:T(8,128)(2,1)S(1)} %pad_maximum_fusion.1), channel_id=1, source_target_pairs={{0,512},{16,528},{32,544},{48,560},{64,576},{80,592},{96,608},{112... | collective-permute-start | bytes 393224 | tf_op jit(solution)/shard_map/ppermute | solution.py:15
  322.0 3.5 gather_fusion.7
  325.5 22.2 %collective-permute-done.7 = bf16[2,16,2048]{2,1,0:T(8,128)(2,1)} collective-permute-done((bf16[2,16,2048]{2,1,0:T(8,128)(2,1)S(1)}, bf16[2,16,2048]{2,1,0:T(8,128)(2,1)}, u32[]{:S(2)}, u32[]{:S(2)}) %collective-permute-start.7) | collective-permute-done | bytes 131104 | tf_op jit(solution)/shard_map/ppermute | solution.py:15
  350.5 4.8 scatter_custom_fusion.4
  355.6 10.5 %scatter_custom_fusion.5 = f32[256,2048]{1,0:T(8,128)} fusion(s32[144]{0:T(256)} %copy-done.6, f32[]{:T(128)} %constant.138.clone.1, pred[144]{0:T(512)(128)(4,1)S(1)} %copy-done.3, pred[144]{0:T(512)(128)(4,1)S(1)} %copy-done.4, bf16[]{:T(256)} %constant.201.clone.1, bf16[16,2048]{1,0:T(8,128)(2,1)S(1)} %get-tuple-element.28, s32[1024]{0:T(1024)S(1)} %pad_clamp_fusion, ...), kind=kCustom, calls=%fused_computation.38 | custom fusion | flops 2064384 | bytes 2696480 | tf_op jit(solution)/shard_map/scatter-add | solution.py:183
  368.0 2.0 fusion.16
  371.8 65.9 %all-reduce = f32[256,8]{1,0:T(8,128)S(1)} all-reduce(f32[256,8]{1,0:T(8,128)S(1)} %reshape.386), channel_id=4, replica_groups=mesh['dp'=64,'expert'=16] {'expert'}, use_global_device_ids=true, to_apply=%region_13.21.clone | all-reduce | flops 2048 | bytes 16384
  438.3 34.9 %reduce-scatter.3.cloned.1.call-done = f32[16,2048]{1,0:T(8,128)} async-done(((f32[256,2048]{1,0:T(8,128)}), f32[16,2048]{1,0:T(8,128)}) %reduce-scatter.3.cloned.1.call-update) | async-done | bytes 131088 | tf_op jit(solution)/shard_map/reduce_scatter | solution.py:192
  474.8 114.1 %reduce-scatter.5.cloned.1.call-done = f32[16,2048]{1,0:T(8,128)} async-done(((f32[256,2048]{1,0:T(8,128)}), f32[16,2048]{1,0:T(8,128)}) %reduce-scatter.5.cloned.1.call-update) | async-done | bytes 131088 | tf_op jit(solution)/shard_map/reduce_scatter | solution.py:193
  (107 shorter events, 43.7 us)
Async XLA Ops:
  7.2 265.7 %copy-start = (bf16[1,2048,768]{2,1,0:T(8,128)(2,1)S(1)}, bf16[1,2048,768]{2,1,0:T(8,128)(2,1)}, u32[]{:S(2)}) copy-start(bf16[1,2048,768]{2,1,0:T(8,128)(2,1)} %param.29) | copy-start | bytes 9437188
  7.2 90.6 %all-gather.5.cloned.1.call-start = ((), (), s32[]{:S(2)}) async-start(), calls=%async_computation.2 | async-start | bytes 1114112 | tf_op jit(solution)/shard_map/all_gather | solution.py:127
  7.9 172.2 %all-gather.7.cloned.1.call-start = ((), (), s32[]{:S(2)}) async-start(), calls=%async_computation.3 | async-start | bytes 1114112 | tf_op jit(solution)/shard_map/all_gather | solution.py:128
  8.7 464.6 %reduce-scatter.3.cloned.1.call-start = ((), (), s32[]{:S(2)}) async-start(), calls=%async_computation.4 | async-start | bytes 2228224 | tf_op jit(solution)/shard_map/reduce_scatter | solution.py:192
  53.4 1.3 copy-start.5
  80.8 0.6 copy-start.6
  187.9 30.9 %collective-permute-start.5 = (bf16[2,16,2048]{2,1,0:T(8,128)(2,1)S(1)}, bf16[2,16,2048]{2,1,0:T(8,128)(2,1)S(1)}, u32[]{:S(2)}, u32[]{:S(2)}) collective-permute-start(bf16[2,16,2048]{2,1,0:T(8,128)(2,1)S(1)} %pad_maximum_fusion), channel_id=1, source_target_pairs={{0,16},{16,0},{32,48},{48,32},{64,80},{80,64},{96,112},{112,96},{1... | collective-permute-start | bytes 393224 | tf_op jit(solution)/shard_map/ppermute | solution.py:15
  190.4 43.2 %collective-permute-start.4 = (bf16[2,16,2048]{2,1,0:T(8,128)(2,1)S(1)}, bf16[2,16,2048]{2,1,0:T(8,128)(2,1)S(1)}, u32[]{:S(2)}, u32[]{:S(2)}) collective-permute-start(bf16[2,16,2048]{2,1,0:T(8,128)(2,1)S(1)} %pad_maximum_fusion), channel_id=1, source_target_pairs={{0,32},{16,48},{32,0},{48,16},{64,96},{80,112},{96,64},{112,80},{1... | collective-permute-start | bytes 393224 | tf_op jit(solution)/shard_map/ppermute | solution.py:15
  193.9 39.8 %collective-permute-start.3 = (bf16[2,16,2048]{2,1,0:T(8,128)(2,1)S(1)}, bf16[2,16,2048]{2,1,0:T(8,128)(2,1)}, u32[]{:S(2)}, u32[]{:S(2)}) collective-permute-start(bf16[2,16,2048]{2,1,0:T(8,128)(2,1)S(1)} %pad_maximum_fusion), channel_id=1, source_target_pairs={{0,64},{16,80},{32,96},{48,112},{64,0},{80,16},{96,32},{112,48},{1... | collective-permute-start | bytes 393224 | tf_op jit(solution)/shard_map/ppermute | solution.py:15
  198.3 35.3 %collective-permute-start.2 = (bf16[2,16,2048]{2,1,0:T(8,128)(2,1)S(1)}, bf16[2,16,2048]{2,1,0:T(8,128)(2,1)}, u32[]{:S(2)}, u32[]{:S(2)}) collective-permute-start(bf16[2,16,2048]{2,1,0:T(8,128)(2,1)S(1)} %pad_maximum_fusion), channel_id=1, source_target_pairs={{0,128},{16,144},{32,160},{48,176},{64,192},{80,208},{96,224},{112... | collective-permute-start | bytes 393224 | tf_op jit(solution)/shard_map/ppermute | solution.py:15
  206.0 58.1 %collective-permute-start.1 = (bf16[2,16,2048]{2,1,0:T(8,128)(2,1)S(1)}, bf16[2,16,2048]{2,1,0:T(8,128)(2,1)}, u32[]{:S(2)}, u32[]{:S(2)}) collective-permute-start(bf16[2,16,2048]{2,1,0:T(8,128)(2,1)S(1)} %pad_maximum_fusion), channel_id=1, source_target_pairs={{0,256},{16,272},{32,288},{48,304},{64,320},{80,336},{96,352},{112... | collective-permute-start | bytes 393224 | tf_op jit(solution)/shard_map/ppermute | solution.py:15
  218.8 45.3 %collective-permute-start = (bf16[2,16,2048]{2,1,0:T(8,128)(2,1)S(1)}, bf16[2,16,2048]{2,1,0:T(8,128)(2,1)}, u32[]{:S(2)}, u32[]{:S(2)}) collective-permute-start(bf16[2,16,2048]{2,1,0:T(8,128)(2,1)S(1)} %pad_maximum_fusion), channel_id=1, source_target_pairs={{0,512},{16,528},{32,544},{48,560},{64,576},{80,592},{96,608},{112... | collective-permute-start | bytes 393224 | tf_op jit(solution)/shard_map/ppermute | solution.py:15
  266.9 1.7 copy-start.8
  266.9 1.7 copy-start.9
  272.9 2.0 copy-start.1
  272.9 2.0 copy-start.2
  278.3 7.8 %copy-start.7 = (pred[16]{0:T(512)(128)(4,1)S(1)}, pred[16]{0:T(512)(128)(4,1)}, u32[]{:S(2)}) copy-start(pred[16]{0:T(512)(128)(4,1)} %get-tuple-element.16) | copy-start | bytes 52
  286.1 23.9 %collective-permute-start.11 = (bf16[2,16,2048]{2,1,0:T(8,128)(2,1)S(1)}, bf16[2,16,2048]{2,1,0:T(8,128)(2,1)S(1)}, u32[]{:S(2)}, u32[]{:S(2)}) collective-permute-start(bf16[2,16,2048]{2,1,0:T(8,128)(2,1)S(1)} %pad_maximum_fusion.1), channel_id=1, source_target_pairs={{0,16},{16,0},{32,48},{48,32},{64,80},{80,64},{96,112},{112,96},{1... | collective-permute-start | bytes 393224 | tf_op jit(solution)/shard_map/ppermute | solution.py:15
  288.7 36.7 %collective-permute-start.10 = (bf16[2,16,2048]{2,1,0:T(8,128)(2,1)S(1)}, bf16[2,16,2048]{2,1,0:T(8,128)(2,1)S(1)}, u32[]{:S(2)}, u32[]{:S(2)}) collective-permute-start(bf16[2,16,2048]{2,1,0:T(8,128)(2,1)S(1)} %pad_maximum_fusion.1), channel_id=1, source_target_pairs={{0,32},{16,48},{32,0},{48,16},{64,96},{80,112},{96,64},{112,80},{1... | collective-permute-start | bytes 393224 | tf_op jit(solution)/shard_map/ppermute | solution.py:15
  290.7 34.8 %collective-permute-start.9 = (bf16[2,16,2048]{2,1,0:T(8,128)(2,1)S(1)}, bf16[2,16,2048]{2,1,0:T(8,128)(2,1)}, u32[]{:S(2)}, u32[]{:S(2)}) collective-permute-start(bf16[2,16,2048]{2,1,0:T(8,128)(2,1)S(1)} %pad_maximum_fusion.1), channel_id=1, source_target_pairs={{0,64},{16,80},{32,96},{48,112},{64,0},{80,16},{96,32},{112,48},{1... | collective-permute-start | bytes 393224 | tf_op jit(solution)/shard_map/ppermute | solution.py:15
  292.6 32.9 %collective-permute-start.8 = (bf16[2,16,2048]{2,1,0:T(8,128)(2,1)S(1)}, bf16[2,16,2048]{2,1,0:T(8,128)(2,1)}, u32[]{:S(2)}, u32[]{:S(2)}) collective-permute-start(bf16[2,16,2048]{2,1,0:T(8,128)(2,1)S(1)} %pad_maximum_fusion.1), channel_id=1, source_target_pairs={{0,128},{16,144},{32,160},{48,176},{64,192},{80,208},{96,224},{112... | collective-permute-start | bytes 393224 | tf_op jit(solution)/shard_map/ppermute | solution.py:15
  303.0 44.7 %collective-permute-start.7 = (bf16[2,16,2048]{2,1,0:T(8,128)(2,1)S(1)}, bf16[2,16,2048]{2,1,0:T(8,128)(2,1)}, u32[]{:S(2)}, u32[]{:S(2)}) collective-permute-start(bf16[2,16,2048]{2,1,0:T(8,128)(2,1)S(1)} %pad_maximum_fusion.1), channel_id=1, source_target_pairs={{0,256},{16,272},{32,288},{48,304},{64,320},{80,336},{96,352},{112... | collective-permute-start | bytes 393224 | tf_op jit(solution)/shard_map/ppermute | solution.py:15
  310.1 37.6 %collective-permute-start.6 = (bf16[2,16,2048]{2,1,0:T(8,128)(2,1)S(1)}, bf16[2,16,2048]{2,1,0:T(8,128)(2,1)}, u32[]{:S(2)}, u32[]{:S(2)}) collective-permute-start(bf16[2,16,2048]{2,1,0:T(8,128)(2,1)S(1)} %pad_maximum_fusion.1), channel_id=1, source_target_pairs={{0,512},{16,528},{32,544},{48,560},{64,576},{80,592},{96,608},{112... | collective-permute-start | bytes 393224 | tf_op jit(solution)/shard_map/ppermute | solution.py:15
  348.6 1.9 copy-start.3
  348.6 1.9 copy-start.4
  355.3 233.6 %reduce-scatter.5.cloned.1.call-start = ((), (), s32[]{:S(2)}) async-start(), calls=%async_computation.5 | async-start | bytes 2228224 | tf_op jit(solution)/shard_map/reduce_scatter | solution.py:193
Sparse Core Ops, SparseCore 0:
  12.2 85.5 all-gather.4
  102.0 78.0 all-gather.6
  355.4 117.7 reduce-scatter.2
  479.2 109.6 reduce-scatter.4
where the time goes:
time: 598 us; the launch traced here: 597 us
  waiting for transfers between devices  294 us (49%)
  blocking collectives  120 us (20%)
  starting transfers between devices  70.8 us (12%)
  local copies, waits for them, and re-layouts  46.3 us (8%)
  other arithmetic  35.6 us (6%)
  between operations  16.9 us (3%)
  matrix products  13.5 us (2%)
    reduce_scatter x1, waiting for transfers between devices, body(): lax.psum_scatter(grad_terms, 'expert', scatter_dimension=0, tiled=True)  114 us
    all_gather x1, waiting for transfers between devices, body(): lax.all_gather(grad_out, 'expert', axis=0, tiled=True)  74.7 us
    ppermute x12, starting transfers between devices, swapped(): lax.ppermute(shard, axis, [(i, i ^ 1 << apart) for i in range(lax.axis_si...  70.4 us
    unnamed x1, blocking collectives  65.9 us
    ppermute x12, waiting for transfers between devices, swapped(): lax.ppermute(shard, axis, [(i, i ^ 1 << apart) for i in range(lax.axis_si...  52.7 us
    reduce_scatter x1, waiting for transfers between devices, body(): lax.psum_scatter(out_terms, 'expert', scatter_dimension=0, tiled=True)  34.9 us
    all_gather x1, blocking collectives, body(): lax.all_gather(routes.astype(jnp.bfloat16), 'expert', axis=0, tiled=True)  33.4 us
    gather x12, local copies, waits for them, and re-layouts, pick_rows(): return jnp.take(table, index, axis=0, mode='fill', fill_value=0)  30.4 us
  transfers between devices with their start and end apart: 16, of which 6 were waited for; matrix products, arithmetic and copies ran while one was open for 9% of the time, Pallas kernels for 0%

commit v1 on v0

v1 whole, which is shorter than its diff:
```python
import functools

import jax
import jax.numpy as jnp
from jax import lax
from jax.experimental import pallas as pl
from jax.experimental.pallas import tpu as pltpu
from jax.sharding import PartitionSpec as P

TOPK = 8
OVF = 16
MEMBERS = 16
TOK = 16
PARTS = 4
ROWS = MEMBERS * TOK
HALF = ROWS // 2
TILE = 256
CHUNK = 32
LANES = 128
MESH = pl.DeviceIdType.MESH

ORDER = [[(q + s) % 4 for s in range(4)] for q in range(PARTS)]


def slot_of(q, p):
    return sum(1 << ORDER[q][s] for s in range(4) if p >> s & 1)


PLACE = [{slot_of(q, p): p for p in range(MEMBERS)} for q in range(PARTS)]
SLOT = [[slot_of(q, p) for p in range(MEMBERS)] for q in range(PARTS)]
STEP_AT = [0, 128, 192, 224]
STEP_ROWS = [128, 64, 32, 16]


def flip(v, bits):
    if bits & 2:
        v = 3 - v
    if bits & 1:
        v = v + 1 - 2 * lax.rem(v, 2)
    return v


def recode(v):
    return v ^ ((v >> 1) & 5)


def nt_dot(a, b):
    return lax.dot_general(a, b, (((1,), (1,)), ((), ())), preferred_element_type=jnp.float32)


def nn_dot(a, b):
    return jnp.dot(a, b, preferred_element_type=jnp.float32)


def kernel(
    levels,
    tokens,
    grads,
    gates,
    routes,
    capacity,
    pair_mask,
    gate_up,
    down,
    out_ref,
    igrad_ref,
    ggrad_ref,
    gu_v,
    dn_v,
    xb,
    sb,
    rb,
    acc,
    p1,
    p2,
    p3,
    hid,
    dpre,
    ta,
    tb,
    gsend,
    grecv,
    gmat,
    gkeep,
    gcol,
    ggacc,
    qsend,
    qrecv,
    dsend,
    drecv,
    local_sem,
    weight_sem,
    ag_send,
    ag_recv,
    rs_send,
    rs_recv,
    g_send,
    g_recv,
    q_send,
    q_recv,
    d_send,
    d_recv,
):
    width = tokens.shape[1]
    part = width // PARTS
    hidden = down.shape[2]
    dp = lax.axis_index("dp")
    me = lax.axis_index("expert")
    mx, my = lax.div(me, 4), lax.rem(me, 4)

    def member(j):
        return (dp, flip(mx, j >> 2) * 4 + flip(my, j & 3))

    def partner(b):
        step = 1 << b
        return (dp + step * (1 - 2 * lax.rem(lax.div(dp, step), 2)), me)

    barrier = pltpu.get_barrier_semaphore()
    everyone = [member(j) for j in range(1, MEMBERS)] + [partner(b) for b in range(levels)]
    for other in everyone:
        pl.semaphore_signal(barrier, inc=1, device_id=other, device_id_type=MESH)

    sources = (tokens, grads)
    local = []
    for a in range(2):
        for q in range(PARTS):
            copy = pltpu.make_async_copy(
                sources[a].at[:, q * part : (q + 1) * part],
                xb.at[a * PARTS + q, 0:TOK, :],
                local_sem.at[a * PARTS + q],
            )
            copy.start()
            local.append(copy)
    weights = []
    for i in range(PARTS):
        rows = slice(i * part, (i + 1) * part)
        weights.append(
            pltpu.make_async_copy(gate_up.at[0, rows, :], gu_v.at[rows, :], weight_sem.at[i])
        )
    for i in range(PARTS):
        rows = slice(i * part, (i + 1) * part)
        weights.append(
            pltpu.make_async_copy(down.at[0, rows, :], dn_v.at[rows, :], weight_sem.at[4 + i])
        )
    for copy in weights:
        copy.start()

    my_code = recode(me)
    rel = recode(routes[...]) ^ my_code
    lane = lax.broadcasted_iota(jnp.int32, (TOK, LANES), 1)
    sub = lax.broadcasted_iota(jnp.int32, (TOK, LANES), 0)
    gate_values = gates[...].astype(jnp.float32)
    dense = jnp.zeros((TOK, LANES), jnp.float32)
    for k in range(TOPK):
        dense += jnp.where(lane == rel[:, k : k + 1], gate_values[:, k : k + 1], 0.0)
    square = jnp.concatenate([dense, jnp.zeros((LANES - TOK, LANES), jnp.float32)], axis=0)
    turned = square.T
    for j in range(MEMBERS):
        gsend[j] = turned[j : j + 1, :]

    pl.semaphore_wait(barrier, len(everyone))

    def gather(a, q, s):
        n = a * PARTS + q
        held = TOK << s
        if s == 0:
            src = sources[a].at[:, q * part : (q + 1) * part]
        else:
            src = xb.at[n, 0:held, :]
        return pltpu.make_async_remote_copy(
            src_ref=src,
            dst_ref=xb.at[n, held : 2 * held, :],
            send_sem=ag_send.at[n * 4 + s],
            recv_sem=ag_recv.at[n * 4 + s],
            device_id=member(1 << ORDER[q][s]),
            device_id_type=MESH,
        )

    def small(src, dst, send, recv, index, slot, other):
        return pltpu.make_async_remote_copy(
            src_ref=src.at[index],
            dst_ref=dst.at[slot],
            send_sem=send.at[slot],
            recv_sem=recv.at[slot],
            device_id=other,
            device_id_type=MESH,
        )

    gates_to = [small(gsend, grecv, g_send, g_recv, j, j, member(j)) for j in range(1, MEMBERS)]
    spare_to = [small(dsend, drecv, d_send, d_recv, 0, b, partner(b)) for b in range(levels)]
    quot_to = [small(qsend, qrecv, q_send, q_recv, j, j, member(j)) for j in range(1, MEMBERS)]

    for a in range(2):
        for q in range(PARTS):
            gather(a, q, 0).start()
    for copy in gates_to:
        copy.start()
    for copy in local:
        copy.wait()
    for s in range(1, 4):
        for a in range(2):
            if (a, s) == (1, 3):
                break
            for q in range(PARTS):
                gather(a, q, s - 1).wait_recv()
                gather(a, q, s).start()

    gmat[0:1, :] = gsend[0]
    for j in range(1, MEMBERS):
        gates_to[j - 1].wait_recv()
        gmat[j : j + 1, :] = grecv[j]
    mat = gmat[...]
    named = jnp.where(mat > 0.0, 1.0, 0.0)
    named16 = named.astype(jnp.bfloat16)
    big0 = lax.broadcasted_iota(jnp.int32, (LANES, LANES), 0)
    big1 = lax.broadcasted_iota(jnp.int32, (LANES, LANES), 1)
    ahead = jnp.where(big0 < big1, 1.0, 0.0).astype(jnp.bfloat16)
    within = nn_dot(named16, ahead)
    counts = nn_dot(named16, jnp.ones((LANES, LANES), jnp.bfloat16)).astype(jnp.bfloat16)
    row_home = recode(lax.broadcasted_iota(jnp.int32, (MEMBERS, MEMBERS), 0) ^ my_code)
    col_home = recode(lax.broadcasted_iota(jnp.int32, (MEMBERS, MEMBERS), 1) ^ my_code)
    earlier = jnp.where(col_home < row_home, 1.0, 0.0).astype(jnp.bfloat16)
    position = within + nn_dot(earlier, counts)
    load = nn_dot(jnp.ones((MEMBERS, MEMBERS), jnp.bfloat16), counts)
    cap = capacity[0, 0].astype(jnp.float32)
    taken = jnp.minimum(cap - jnp.minimum(load, cap), float(OVF))
    dsend[0] = taken[0:1, :]
    for copy in spare_to:
        copy.start()

    for q in range(PARTS):
        gather(1, q, 2).wait_recv()
        gather(1, q, 3).start()

    limit = jnp.zeros((1, LANES), jnp.float32) + cap
    for b in range(levels):
        spare_to[b].wait_recv()
        limit += drecv[b] * (pair_mask[0] == 1 << b).astype(jnp.float32)
    gkeep[...] = jnp.where(position < limit, mat, 0.0)
    for j in range(MEMBERS):
        row = jnp.broadcast_to(gkeep[j : j + 1, :], (TOK, LANES))
        column = jnp.sum(jnp.where(lane == sub, row, 0.0), axis=1, keepdims=True)
        gcol[j * TOK : (j + 1) * TOK, :] = jnp.broadcast_to(column, (TOK, LANES))

    for q in range(PARTS):
        gather(0, q, 3).wait_recv()
    for copy in weights[:4]:
        copy.wait()

    def block(a, q):
        pieces = []
        for j in range(MEMBERS):
            p = PLACE[q][j]
            pieces.append(xb[a * PARTS + q, p * TOK : (p + 1) * TOK, :])
        return jnp.concatenate(pieces, axis=0)

    def forward_tile(n, carry):
        at = pl.multiple_of(n * TILE, TILE)
        up_at = pl.multiple_of(hidden + n * TILE, TILE)
        gate_pre = jnp.zeros((ROWS, TILE), jnp.float32)
        up_pre = jnp.zeros((ROWS, TILE), jnp.float32)
        for q in range(PARTS):
            lhs = block(0, q)
            rows = slice(q * part, (q + 1) * part)
            gate_pre += nn_dot(lhs, gu_v[rows, pl.ds(at, TILE)])
            up_pre += nn_dot(lhs, gu_v[rows, pl.ds(up_at, TILE)])
        ta[...] = gate_pre
        tb[...] = up_pre

        def rows_of(i, inner):
            rows = pl.ds(pl.multiple_of(i * CHUNK, CHUNK), CHUNK)
            a = ta[rows, :]
            b = tb[rows, :]
            sigma = jax.nn.sigmoid(a)
            swish = a * sigma
            both = swish * b
            cols = pl.ds(at, TILE)
            p1[rows, cols] = both
            p2[rows, cols] = swish
            p3[rows, cols] = b * sigma * (1.0 + a * (1.0 - sigma))
            g = gcol[rows, :]
            hid[rows, cols] = (both * jnp.concatenate([g, g], axis=1)).astype(jnp.bfloat16)
            return inner

        return lax.fori_loop(0, ROWS // CHUNK, rows_of, carry)

    lax.fori_loop(0, hidden // TILE, forward_tile, 0)

    def reduce(a, q, r):
        n = a * PARTS + q
        rows = slice(STEP_AT[r], STEP_AT[r] + STEP_ROWS[r])
        return pltpu.make_async_remote_copy(
            src_ref=sb.at[n, rows, :],
            dst_ref=rb.at[n, rows, :],
            send_sem=rs_send.at[n * 4 + r],
            recv_sem=rs_recv.at[n * 4 + r],
            device_id=member(1 << ORDER[q][3 - r]),
            device_id_type=MESH,
        )

    def permuted(ref, q):
        return jnp.concatenate(
            [ref[SLOT[q][p] * TOK : (SLOT[q][p] + 1) * TOK, :] for p in range(MEMBERS)], axis=0
        )

    def produce(a, q, ref, weight):
        n = a * PARTS + q
        tile = min(TILE, part)
        for c in range(part // tile):
            cols = slice(c * tile, (c + 1) * tile)
            rows = slice(q * part + c * tile, q * part + (c + 1) * tile)
            value = nt_dot(permuted(ref, q), weight[rows, :])
            sb[n, 0:HALF, cols] = value[HALF:, :].astype(jnp.bfloat16)
            acc[n, :, cols] = value[:HALF, :]
        reduce(a, q, 0).start()

    def pass_on(a, q, r):
        n = a * PARTS + q
        reduce(a, q, r - 1).wait_recv()
        size = STEP_ROWS[r]
        total = acc[n, size : 2 * size, :]
        for i in range(r):
            at = STEP_AT[i] + size
            total += rb[n, at : at + size, :].astype(jnp.float32)
        sb[n, STEP_AT[r] : STEP_AT[r] + size, :] = total.astype(jnp.bfloat16)
        reduce(a, q, r).start()

    def finish(a, q, ref):
        n = a * PARTS + q
        reduce(a, q, 3).wait_recv()
        total = acc[n, 0:TOK, :]
        for i in range(4):
            total += rb[n, STEP_AT[i] : STEP_AT[i] + TOK, :].astype(jnp.float32)
        ref[:, q * part : (q + 1) * part] = total.astype(jnp.bfloat16)

    for copy in weights[4:]:
        copy.wait()
    for q in range(PARTS):
        produce(0, q, hid, dn_v)

    for q in range(PARTS):
        gather(1, q, 3).wait_recv()
    ggacc[...] = jnp.zeros_like(ggacc)

    def backward_tile(n, carry):
        at = pl.multiple_of(n * TILE, TILE)
        up_at = pl.multiple_of(hidden + n * TILE, TILE)
        total = jnp.zeros((ROWS, TILE), jnp.float32)
        for q in range(PARTS):
            total += nn_dot(block(1, q), dn_v[q * part : (q + 1) * part, pl.ds(at, TILE)])
        ta[...] = total

        def rows_of(i, inner):
            rows = pl.ds(pl.multiple_of(i * CHUNK, CHUNK), CHUNK)
            cols = pl.ds(at, TILE)
            back = ta[rows, :]
            inner_terms = back * p1[rows, cols]
            ggacc[rows, :] += inner_terms[:, :LANES] + inner_terms[:, LANES:]
            g = gcol[rows, :]
            scaled = back * jnp.concatenate([g, g], axis=1)
            dpre[rows, cols] = (scaled * p3[rows, cols]).astype(jnp.bfloat16)
            dpre[rows, pl.ds(up_at, TILE)] = (scaled * p2[rows, cols]).astype(jnp.bfloat16)
            return inner

        return lax.fori_loop(0, ROWS // CHUNK, rows_of, carry)

    lax.fori_loop(0, hidden // TILE, backward_tile, 0)

    for q in range(PARTS):
        produce(1, q, dpre, gu_v)

    for j in range(MEMBERS):
        column = jnp.sum(ggacc[j * TOK : (j + 1) * TOK, :], axis=1, keepdims=True)
        row = jnp.sum(jnp.where(lane == sub, column, 0.0), axis=0, keepdims=True)
        qsend[j] = jnp.where(gkeep[j : j + 1, :] > 0.0, row, 0.0)
    for copy in quot_to:
        copy.start()

    for r in range(1, 4):
        for q in range(PARTS):
            pass_on(0, q, r)
        for q in range(PARTS):
            pass_on(1, q, r)

    gmat[0:1, :] = qsend[0]
    for j in range(1, MEMBERS):
        quot_to[j - 1].wait_recv()
        gmat[j : j + 1, :] = qrecv[j]
    square = jnp.concatenate(
        [gmat[...], jnp.zeros((LANES - MEMBERS, LANES), jnp.float32)], axis=0
    )
    by_token = square.T[:TOK, :]
    picked = jnp.zeros((TOK, LANES), jnp.float32)
    for k in range(TOPK):
        value = jnp.sum(
            jnp.where(lane == rel[:, k : k + 1], by_token, 0.0), axis=1, keepdims=True
        )
        picked += jnp.where(lane == k, value, 0.0)
    ggrad_ref[...] = picked[:, :TOPK]

    for q in range(PARTS):
        finish(0, q, out_ref)
    for q in range(PARTS):
        finish(1, q, igrad_ref)

    for a in range(2):
        for q in range(PARTS):
            for s in range(4):
                gather(a, q, s).wait_send()
                reduce(a, q, s).wait_send()
    for copy in gates_to + spare_to + quot_to:
        copy.wait_send()


def body(tokens, grad_out, gate_probs, routes, capacity, pair_mask, gate_up_weight, down_weight):
    width = tokens.shape[1]
    hidden = down_weight.shape[2]
    part = width // PARTS
    levels = lax.axis_size("dp").bit_length() - 1
    vmem = pl.BlockSpec(memory_space=pltpu.VMEM)
    smem = pl.BlockSpec(memory_space=pltpu.SMEM)
    anywhere = pl.BlockSpec(memory_space=pl.ANY)
    f32, b16 = jnp.float32, jnp.bfloat16
    dma = pltpu.SemaphoreType.DMA
    streams = 2 * PARTS
    return pl.pallas_call(
        functools.partial(kernel, levels),
        out_shape=(
            jax.ShapeDtypeStruct((TOK, width), b16),
            jax.ShapeDtypeStruct((TOK, width), b16),
            jax.ShapeDtypeStruct((TOK, TOPK), f32),
        ),
        in_specs=[anywhere, anywhere, vmem, vmem, smem, smem, anywhere, anywhere],
        out_specs=(vmem, vmem, vmem),
        scratch_shapes=[
            pltpu.VMEM((width, 2 * hidden), b16),
            pltpu.VMEM((width, hidden), b16),
            pltpu.VMEM((streams, ROWS, part), b16),
            pltpu.VMEM((streams, 240, part), b16),
            pltpu.VMEM((streams, 240, part), b16),
            pltpu.VMEM((streams, HALF, part), f32),
            pltpu.VMEM((ROWS, hidden), f32),
            pltpu.VMEM((ROWS, hidden), f32),
            pltpu.VMEM((ROWS, hidden), f32),
            pltpu.VMEM((ROWS, hidden), b16),
            pltpu.VMEM((ROWS, 2 * hidden), b16),
            pltpu.VMEM((ROWS, TILE), f32),
            pltpu.VMEM((ROWS, TILE), f32),
            pltpu.VMEM((MEMBERS, 1, LANES), f32),
            pltpu.VMEM((MEMBERS, 1, LANES), f32),
            pltpu.VMEM((MEMBERS, LANES), f32),
            pltpu.VMEM((MEMBERS, LANES), f32),
            pltpu.VMEM((ROWS, LANES), f32),
            pltpu.VMEM((ROWS, LANES), f32),
            pltpu.VMEM((MEMBERS, 1, LANES), f32),
            pltpu.VMEM((MEMBERS, 1, LANES), f32),
            pltpu.VMEM((1, 1, LANES), f32),
            pltpu.VMEM((max(levels, 1), 1, LANES), f32),
            dma((streams,)),
            dma((8,)),
            dma((streams * 4,)),
            dma((streams * 4,)),
            dma((streams * 4,)),
            dma((streams * 4,)),
            dma((MEMBERS,)),
            dma((MEMBERS,)),
            dma((MEMBERS,)),
            dma((MEMBERS,)),
            dma((max(levels, 1),)),
            dma((max(levels, 1),)),
        ],
        compiler_params=pltpu.CompilerParams(
            collective_id=0, has_side_effects=True, vmem_limit_bytes=48 * 1024 * 1024
        ),
        cost_estimate=pl.CostEstimate(
            flops=2 * ROWS * width * hidden * 6,
            bytes_accessed=width * hidden * 6,
            transcendentals=ROWS * hidden,
        ),
    )(tokens, grad_out, gate_probs, routes, capacity, pair_mask, gate_up_weight, down_weight)


def solution(mesh):
    rows = P(("dp", "expert"), None)
    return jax.shard_map(
        body,
        mesh=mesh,
        in_specs=(
            rows,
            rows,
            rows,
            rows,
            P("dp", "expert"),
            P("expert"),
            P("expert", None, None),
            P("expert", None, None),
        ),
        out_specs=(rows, rows, rows),
        check_vma=False,
    )
```

time: 598 us -> 82.7 us (0.14)
  the two profiles are of different devices: /device:TPU:6 before, /device:TPU:8 now
where the time goes in v1:
time: 82.7 us; the launch traced here: 82.3 us
  Pallas kernels  73.4 us (89%)
  local copies, waits for them, and re-layouts  7 us (8%)
  between operations  1.94 us (2%)
    pallas_call x1, Pallas kernels, body(): pl.pallas_call(functools.partial(kernel, levels), out_shape=(jax.ShapeDty...  73.4 us
    unnamed x10, local copies, waits for them, and re-layouts  6.34 us

profile of v1, /device:TPU:8, one launch (start us, length us, event | category | flops | bytes accessed | tf_op | source)
XLA Modules:
  0.0 82.3 jit_solution(14900555095646975260)
XLA Ops:
  1.9 0.8 copy.11.gates
  2.7 0.8 copy.12.routes
  3.4 0.0 copy-start
  3.4 1.9 %copy-done = bf16[1,2048,768]{2,1,0:T(8,128)(2,1)S(1)} copy-done((bf16[1,2048,768]{2,1,0:T(8,128)(2,1)S(1)}, bf16[1,2048,768]{2,1,0:T(8,128)(2,1)}, u32[]{:S(2)}) %copy-start) | copy-done | bytes 3145752
  5.3 0.0 copy-start.1
  5.3 0.8 %copy-done.1 = bf16[16,2048]{1,0:T(8,128)(2,1)S(1)} copy-done((bf16[16,2048]{1,0:T(8,128)(2,1)S(1)}, bf16[16,2048]{1,0:T(8,128)(2,1)}, u32[]{:S(2)}) %copy-start.1) | copy-done | bytes 65560
  6.2 0.0 copy-start.2
  6.2 0.8 %copy-done.2 = bf16[16,2048]{1,0:T(8,128)(2,1)S(1)} copy-done((bf16[16,2048]{1,0:T(8,128)(2,1)S(1)}, bf16[16,2048]{1,0:T(8,128)(2,1)}, u32[]{:S(2)}) %copy-start.2) | copy-done | bytes 65560
  7.0 73.4 %shard_map.103 = (bf16[16,2048]{1,0:T(8,128)(2,1)S(1)}, bf16[16,2048]{1,0:T(8,128)(2,1)S(1)}, f32[16,8]{1,0:T(8,128)S(1)}) custom-call(bf16[16,2048]{1,0:T(8,128)(2,1)S(1)} %copy-done.1, bf16[16,2048]{1,0:T(8,128)(2,1)S(1)} %copy-done.2, bf16[16,8]{1,0:T(8,128)(2,1)S(1)} %copy.11.gates, s32[16,8]{1,0:T(8,128)S(1)} %copy.12.routes, ...), custom_call_target="tpu_custom_call" | custom-call | flops 4831838208 | bytes 9437184 | tf_op jit(solution)/shard_map/pallas_call | solution.py:426
  80.4 0.7 copy.13
  81.0 0.6 copy.18
  81.7 0.6 copy.19
Async XLA Ops:
  3.4 1.9 %copy-start = (bf16[1,2048,768]{2,1,0:T(8,128)(2,1)S(1)}, bf16[1,2048,768]{2,1,0:T(8,128)(2,1)}, u32[]{:S(2)}) copy-start(bf16[1,2048,768]{2,1,0:T(8,128)(2,1)} %down.1) | copy-start | bytes 9437188
  5.3 0.8 %copy-start.1 = (bf16[16,2048]{1,0:T(8,128)(2,1)S(1)}, bf16[16,2048]{1,0:T(8,128)(2,1)}, u32[]{:S(2)}) copy-start(bf16[16,2048]{1,0:T(8,128)(2,1)} %tokens.1) | copy-start | bytes 196612
  6.2 0.8 %copy-start.2 = (bf16[16,2048]{1,0:T(8,128)(2,1)S(1)}, bf16[16,2048]{1,0:T(8,128)(2,1)}, u32[]{:S(2)}) copy-start(bf16[16,2048]{1,0:T(8,128)(2,1)} %grads.1) | copy-start | bytes 196612

commit v2 on v1

--- a/solution.py
+++ b/solution.py
@@ -17,6 +17,7 @@
 TILE = 256
 CHUNK = 32
 LANES = 128
+RING_BIT = 3
 MESH = pl.DeviceIdType.MESH
 
 ORDER = [[(q + s) % 4 for s in range(4)] for q in range(PARTS)]
@@ -71,13 +72,16 @@
     sb,
     rb,
     acc,
-    p1,
     p2,
     p3,
     hid,
     dpre,
     ta,
     tb,
+    gates_v,
+    routes_v,
+    cap_s,
+    mask_s,
     gsend,
     grecv,
     gmat,
@@ -89,6 +93,7 @@
     dsend,
     drecv,
     local_sem,
+    tiny_sem,
     weight_sem,
     ag_send,
     ag_recv,
@@ -104,6 +109,7 @@
     width = tokens.shape[1]
     part = width // PARTS
     hidden = down.shape[2]
+    replicas = 1 << levels
     dp = lax.axis_index("dp")
     me = lax.axis_index("expert")
     mx, my = lax.div(me, 4), lax.rem(me, 4)
@@ -111,12 +117,33 @@
     def member(j):
         return (dp, flip(mx, j >> 2) * 4 + flip(my, j & 3))
 
+    def moved(step):
+        return (lax.rem(dp + step + replicas, replicas), me)
+
     def partner(b):
         step = 1 << b
         return (dp + step * (1 - 2 * lax.rem(lax.div(dp, step), 2)), me)
 
+    direct = min(levels, RING_BIT)
+    jump = 1 << RING_BIT
+    far = (replicas // jump) // 2
+    back_far = far // 2
+    ways = [1] * (far > 0) + [-1] * (back_far > 0)
+
+    tiny = [
+        pltpu.make_async_copy(routes, routes_v, tiny_sem.at[0]),
+        pltpu.make_async_copy(gates, gates_v, tiny_sem.at[1]),
+        pltpu.make_async_copy(capacity, cap_s, tiny_sem.at[2]),
+        pltpu.make_async_copy(pair_mask, mask_s, tiny_sem.at[3]),
+    ]
+    for copy in tiny:
+        copy.start()
     barrier = pltpu.get_barrier_semaphore()
-    everyone = [member(j) for j in range(1, MEMBERS)] + [partner(b) for b in range(levels)]
+    everyone = [member(j) for j in range(1, MEMBERS)] + [partner(b) for b in range(direct)]
+    if far > 1:
+        everyone += [moved(jump), moved(-jump)]
+    elif far:
+        everyone += [moved(jump)]
     for other in everyone:
         pl.semaphore_signal(barrier, inc=1, device_id=other, device_id_type=MESH)
 
@@ -146,17 +173,20 @@
         copy.start()
 
     my_code = recode(me)
-    rel = recode(routes[...]) ^ my_code
     lane = lax.broadcasted_iota(jnp.int32, (TOK, LANES), 1)
     sub = lax.broadcasted_iota(jnp.int32, (TOK, LANES), 0)
-    gate_values = gates[...].astype(jnp.float32)
-    dense = jnp.zeros((TOK, LANES), jnp.float32)
+    slots = lax.broadcasted_iota(jnp.int32, (MEMBERS, TOK), 0)
+    for copy in tiny:
+        copy.wait()
+    rel = recode(routes_v[...]) ^ my_code
+    gate_values = gates_v[...].astype(jnp.float32)
+    dense = jnp.zeros((MEMBERS, TOK), jnp.float32)
     for k in range(TOPK):
-        dense += jnp.where(lane == rel[:, k : k + 1], gate_values[:, k : k + 1], 0.0)
-    square = jnp.concatenate([dense, jnp.zeros((LANES - TOK, LANES), jnp.float32)], axis=0)
-    turned = square.T
+        dense += jnp.where(slots == rel[k : k + 1, :], gate_values[k : k + 1, :], 0.0)
+    gmat[...] = jnp.zeros_like(gmat)
+    gmat[:, 0:TOK] = dense
     for j in range(MEMBERS):
-        gsend[j] = turned[j : j + 1, :]
+        gsend[j] = gmat[j : j + 1, :]
 
     pl.semaphore_wait(barrier, len(everyone))
 
@@ -187,60 +217,73 @@
         )
 
     gates_to = [small(gsend, grecv, g_send, g_recv, j, j, member(j)) for j in range(1, MEMBERS)]
-    spare_to = [small(dsend, drecv, d_send, d_recv, 0, b, partner(b)) for b in range(levels)]
+    direct_to = [small(dsend, drecv, d_send, d_recv, 0, b, partner(b)) for b in range(direct)]
+
+    def ring_slot(way, d):
+        return direct + d - 1 + (far if way < 0 else 0)
+
+    def ring_hop(way, d):
+        src, index = (dsend, 0) if d == 1 else (drecv, ring_slot(way, d - 1))
+        return small(src, drecv, d_send, d_recv, index, ring_slot(way, d), moved(way * jump))
+
+    hops = {(1, d): ring_hop(1, d) for d in range(1, far + 1)}
+    hops.update({(-1, d): ring_hop(-1, d) for d in range(1, back_far + 1)})
+
+    def ring_round(d):
+        for way in ways:
+            if (way, d) in hops:
+                if d > 1:
+                    hops[way, d - 1].wait_recv()
+                hops[way, d].start()
+
     quot_to = [small(qsend, qrecv, q_send, q_recv, j, j, member(j)) for j in range(1, MEMBERS)]
 
-    for a in range(2):
-        for q in range(PARTS):
-            gather(a, q, 0).start()
+    def step_on(a, s):
+        for q in range(PARTS):
+            gather(a, q, s - 1).wait_recv()
+            gather(a, q, s).start()
+
+    for q in range(PARTS):
+        gather(0, q, 0).start()
     for copy in gates_to:
         copy.start()
+    for q in range(PARTS):
+        gather(1, q, 0).start()
     for copy in local:
         copy.wait()
-    for s in range(1, 4):
-        for a in range(2):
-            if (a, s) == (1, 3):
-                break
-            for q in range(PARTS):
-                gather(a, q, s - 1).wait_recv()
-                gather(a, q, s).start()
+    step_on(0, 1)
+    step_on(1, 1)
 
     gmat[0:1, :] = gsend[0]
     for j in range(1, MEMBERS):
         gates_to[j - 1].wait_recv()
         gmat[j : j + 1, :] = grecv[j]
     mat = gmat[...]
-    named = jnp.where(mat > 0.0, 1.0, 0.0)
-    named16 = named.astype(jnp.bfloat16)
+    named16 = jnp.where(mat > 0.0, 1.0, 0.0).astype(jnp.bfloat16)
+    counts = nn_dot(named16, jnp.ones((LANES, LANES), jnp.bfloat16)).astype(jnp.bfloat16)
+    load = nn_dot(jnp.ones((MEMBERS, MEMBERS), jnp.bfloat16), counts)
+    cap = jnp.broadcast_to(cap_s[...].astype(jnp.float32), (1, LANES))
+    taken = jnp.minimum(cap - jnp.minimum(load, cap), float(OVF))
+    dsend[0] = taken[0:1, :]
+    ring_round(1)
+    for copy in direct_to:
+        copy.start()
+
+    step_on(0, 2)
+    step_on(1, 2)
     big0 = lax.broadcasted_iota(jnp.int32, (LANES, LANES), 0)
     big1 = lax.broadcasted_iota(jnp.int32, (LANES, LANES), 1)
     ahead = jnp.where(big0 < big1, 1.0, 0.0).astype(jnp.bfloat16)
     within = nn_dot(named16, ahead)
-    counts = nn_dot(named16, jnp.ones((LANES, LANES), jnp.bfloat16)).astype(jnp.bfloat16)
     row_home = recode(lax.broadcasted_iota(jnp.int32, (MEMBERS, MEMBERS), 0) ^ my_code)
     col_home = recode(lax.broadcasted_iota(jnp.int32, (MEMBERS, MEMBERS), 1) ^ my_code)
     earlier = jnp.where(col_home < row_home, 1.0, 0.0).astype(jnp.bfloat16)
     position = within + nn_dot(earlier, counts)
-    load = nn_dot(jnp.ones((MEMBERS, MEMBERS), jnp.bfloat16), counts)
-    cap = capacity[0, 0].astype(jnp.float32)
-    taken = jnp.minimum(cap - jnp.minimum(load, cap), float(OVF))
-    dsend[0] = taken[0:1, :]
-    for copy in spare_to:
-        copy.start()
-
-    for q in range(PARTS):
-        gather(1, q, 2).wait_recv()
-        gather(1, q, 3).start()
-
-    limit = jnp.zeros((1, LANES), jnp.float32) + cap
-    for b in range(levels):
-        spare_to[b].wait_recv()
-        limit += drecv[b] * (pair_mask[0] == 1 << b).astype(jnp.float32)
-    gkeep[...] = jnp.where(position < limit, mat, 0.0)
-    for j in range(MEMBERS):
-        row = jnp.broadcast_to(gkeep[j : j + 1, :], (TOK, LANES))
-        column = jnp.sum(jnp.where(lane == sub, row, 0.0), axis=1, keepdims=True)
-        gcol[j * TOK : (j + 1) * TOK, :] = jnp.broadcast_to(column, (TOK, LANES))
+    ring_round(2)
+    step_on(0, 3)
+    ring_round(3)
+    step_on(1, 3)
+    ring_round(4)
 
     for q in range(PARTS):
         gather(0, q, 3).wait_recv()
@@ -275,16 +318,35 @@
             swish = a * sigma
             both = swish * b
             cols = pl.ds(at, TILE)
-            p1[rows, cols] = both
             p2[rows, cols] = swish
             p3[rows, cols] = b * sigma * (1.0 + a * (1.0 - sigma))
-            g = gcol[rows, :]
-            hid[rows, cols] = (both * jnp.concatenate([g, g], axis=1)).astype(jnp.bfloat16)
+            hid[rows, cols] = both.astype(jnp.bfloat16)
             return inner
 
         return lax.fori_loop(0, ROWS // CHUNK, rows_of, carry)
 
     lax.fori_loop(0, hidden // TILE, forward_tile, 0)
+
+    limit = jnp.zeros((1, LANES), jnp.float32) + cap
+    for b in range(direct):
+        direct_to[b].wait_recv()
+        limit += drecv[b] * (mask_s[...] == 1 << b).astype(jnp.float32)
+    for way, d in hops:
+        if (way, d + 1) not in hops:
+            hops[way, d].wait_recv()
+    for b in range(direct, levels):
+        d = 1 << (b - direct)
+        wanted = (mask_s[...] == 1 << b).astype(jnp.float32)
+        behind = drecv[ring_slot(1, d)]
+        if d < far:
+            upper = lax.rem(lax.div(dp, 1 << b), 2).astype(jnp.float32)
+            behind = upper * behind + (1.0 - upper) * drecv[ring_slot(-1, d)]
+        limit += wanted * behind
+    gkeep[...] = jnp.where(position < limit, mat, 0.0)
+    for j in range(MEMBERS):
+        row = jnp.broadcast_to(gkeep[j : j + 1, :], (TOK, LANES))
+        column = jnp.sum(jnp.where(lane == sub, row, 0.0), axis=1, keepdims=True)
+        gcol[j * TOK : (j + 1) * TOK, :] = jnp.broadcast_to(column, (TOK, LANES))
 
     def reduce(a, q, r):
         n = a * PARTS + q
@@ -306,10 +368,12 @@
     def produce(a, q, ref, weight):
         n = a * PARTS + q
         tile = min(TILE, part)
+        gate = permuted(gcol, q)
+        gate = jnp.concatenate([gate] * (tile // LANES), axis=1)
         for c in range(part // tile):
             cols = slice(c * tile, (c + 1) * tile)
             rows = slice(q * part + c * tile, q * part + (c + 1) * tile)
-            value = nt_dot(permuted(ref, q), weight[rows, :])
+            value = nt_dot(permuted(ref, q), weight[rows, :]) * gate
             sb[n, 0:HALF, cols] = value[HALF:, :].astype(jnp.bfloat16)
             acc[n, :, cols] = value[:HALF, :]
         reduce(a, q, 0).start()
@@ -354,12 +418,10 @@
             rows = pl.ds(pl.multiple_of(i * CHUNK, CHUNK), CHUNK)
             cols = pl.ds(at, TILE)
             back = ta[rows, :]
-            inner_terms = back * p1[rows, cols]
-            ggacc[rows, :] += inner_terms[:, :LANES] + inner_terms[:, LANES:]
-            g = gcol[rows, :]
-            scaled = back * jnp.concatenate([g, g], axis=1)
-            dpre[rows, cols] = (scaled * p3[rows, cols]).astype(jnp.bfloat16)
-            dpre[rows, pl.ds(up_at, TILE)] = (scaled * p2[rows, cols]).astype(jnp.bfloat16)
+            terms = back * hid[rows, cols].astype(jnp.float32)
+            ggacc[rows, :] += terms[:, :LANES] + terms[:, LANES:]
+            dpre[rows, cols] = (back * p3[rows, cols]).astype(jnp.bfloat16)
+            dpre[rows, pl.ds(up_at, TILE)] = (back * p2[rows, cols]).astype(jnp.bfloat16)
             return inner
 
         return lax.fori_loop(0, ROWS // CHUNK, rows_of, carry)
@@ -386,17 +448,11 @@
     for j in range(1, MEMBERS):
         quot_to[j - 1].wait_recv()
         gmat[j : j + 1, :] = qrecv[j]
-    square = jnp.concatenate(
-        [gmat[...], jnp.zeros((LANES - MEMBERS, LANES), jnp.float32)], axis=0
-    )
-    by_token = square.T[:TOK, :]
-    picked = jnp.zeros((TOK, LANES), jnp.float32)
+    by_slot = gmat[:, 0:TOK]
     for k in range(TOPK):
-        value = jnp.sum(
-            jnp.where(lane == rel[:, k : k + 1], by_token, 0.0), axis=1, keepdims=True
-        )
-        picked += jnp.where(lane == k, value, 0.0)
-    ggrad_ref[...] = picked[:, :TOPK]
+        ggrad_ref[k : k + 1, :] = jnp.sum(
+            jnp.where(slots == rel[k : k + 1, :], by_slot, 0.0), axis=0, keepdims=True
+        )
 
     for q in range(PARTS):
         finish(0, q, out_ref)
@@ -408,7 +464,7 @@
             for s in range(4):
                 gather(a, q, s).wait_send()
                 reduce(a, q, s).wait_send()
-    for copy in gates_to + spare_to + quot_to:
+    for copy in gates_to + direct_to + list(hops.values()) + quot_to:
         copy.wait_send()
 
 
@@ -418,19 +474,18 @@
     part = width // PARTS
     levels = lax.axis_size("dp").bit_length() - 1
     vmem = pl.BlockSpec(memory_space=pltpu.VMEM)
-    smem = pl.BlockSpec(memory_space=pltpu.SMEM)
-    anywhere = pl.BlockSpec(memory_space=pl.ANY)
+    in_hbm = pl.BlockSpec(memory_space=pltpu.HBM)
     f32, b16 = jnp.float32, jnp.bfloat16
     dma = pltpu.SemaphoreType.DMA
     streams = 2 * PARTS
-    return pl.pallas_call(
+    out, igrad, ggrad = pl.pallas_call(
         functools.partial(kernel, levels),
         out_shape=(
             jax.ShapeDtypeStruct((TOK, width), b16),
             jax.ShapeDtypeStruct((TOK, width), b16),
-            jax.ShapeDtypeStruct((TOK, TOPK), f32),
+            jax.ShapeDtypeStruct((TOPK, TOK), f32),
         ),
-        in_specs=[anywhere, anywhere, vmem, vmem, smem, smem, anywhere, anywhere],
+        in_specs=[in_hbm] * 8,
         out_specs=(vmem, vmem, vmem),
         scratch_shapes=[
             pltpu.VMEM((width, 2 * hidden), b16),
@@ -441,11 +496,14 @@
             pltpu.VMEM((streams, HALF, part), f32),
             pltpu.VMEM((ROWS, hidden), f32),
             pltpu.VMEM((ROWS, hidden), f32),
-            pltpu.VMEM((ROWS, hidden), f32),
             pltpu.VMEM((ROWS, hidden), b16),
             pltpu.VMEM((ROWS, 2 * hidden), b16),
             pltpu.VMEM((ROWS, TILE), f32),
             pltpu.VMEM((ROWS, TILE), f32),
+            pltpu.VMEM((TOPK, TOK), b16),
+            pltpu.VMEM((TOPK, TOK), jnp.int32),
+            pltpu.VMEM((1, 1), jnp.int32),
+            pltpu.VMEM((1, 1), jnp.int32),
             pltpu.VMEM((MEMBERS, 1, LANES), f32),
             pltpu.VMEM((MEMBERS, 1, LANES), f32),
             pltpu.VMEM((MEMBERS, LANES), f32),
@@ -455,8 +513,9 @@
             pltpu.VMEM((MEMBERS, 1, LANES), f32),
             pltpu.VMEM((MEMBERS, 1, LANES), f32),
             pltpu.VMEM((1, 1, LANES), f32),
-            pltpu.VMEM((max(levels, 1), 1, LANES), f32),
+            pltpu.VMEM((16, 1, LANES), f32),
             dma((streams,)),
+            dma((4,)),
             dma((8,)),
             dma((streams * 4,)),
             dma((streams * 4,)),
@@ -466,18 +525,28 @@
             dma((MEMBERS,)),
             dma((MEMBERS,)),
             dma((MEMBERS,)),
-            dma((max(levels, 1),)),
-            dma((max(levels, 1),)),
+            dma((16,)),
+            dma((16,)),
         ],
         compiler_params=pltpu.CompilerParams(
-            collective_id=0, has_side_effects=True, vmem_limit_bytes=48 * 1024 * 1024
+            collective_id=0, has_side_effects=True, vmem_limit_bytes=60 * 1024 * 1024
         ),
         cost_estimate=pl.CostEstimate(
             flops=2 * ROWS * width * hidden * 6,
             bytes_accessed=width * hidden * 6,
             transcendentals=ROWS * hidden,
         ),
-    )(tokens, grad_out, gate_probs, routes, capacity, pair_mask, gate_up_weight, down_weight)
+    )(
+        tokens,
+        grad_out,
+        gate_probs.T,
+        routes.T,
+        capacity,
+        pair_mask.reshape(1, 1),
+        gate_up_weight,
+        down_weight,
+    )
+    return (out, igrad, ggrad.T)
 
 
 def solution(mesh):

time: 82.7 us -> 75.6 us (0.914)
  Pallas kernels: 73.4 us -> 69.2 us
  local copies, waits for them, and re-layouts: 7 us -> 4.22 us
    pallas_call x1, Pallas kernels: 73.4 us -> 69.2 us  [body(): pl.pallas_call(functools.partial(kernel, levels), out_shape=(jax.ShapeDty...]
    unnamed x10 -> x3, local copies, waits for them, and re-layouts: 6.34 us -> 4.22 us
where the time goes in v2:
time: 75.6 us; the launch traced here: 75.3 us
  Pallas kernels  69.2 us (92%)
  local copies, waits for them, and re-layouts  4.22 us (6%)
  between operations  1.93 us (3%)
    pallas_call x1, Pallas kernels, body(): pl.pallas_call(functools.partial(kernel, levels), out_shape=(jax.ShapeDty...  69.2 us
    unnamed x3, local copies, waits for them, and re-layouts  4.22 us

profile of v2, /device:TPU:8, one launch (start us, length us, event | category | flops | bytes accessed | tf_op | source)
XLA Modules:
  0.0 75.3 jit_solution(4255122708809231932)
XLA Ops:
  1.9 69.2 %shard_map.103 = (bf16[16,2048]{1,0:T(8,128)(2,1)}, bf16[16,2048]{1,0:T(8,128)(2,1)}, f32[8,16]{1,0:T(8,128)}) custom-call(bf16[16,2048]{1,0:T(8,128)(2,1)} %tokens.1, bf16[16,2048]{1,0:T(8,128)(2,1)} %grads.1, bf16[8,16]{1,0:T(8,128)(2,1)} %bitcast.7, s32[8,16]{1,0:T(8,128)} %bitcast.6, s32[1,1]{1,0:T(1,128)S(6)} %copy.14.capacity, ...), custom_call_target="tpu_custom_call" | custom-call | flops 4831838208 | bytes 9437184 | tf_op jit(solution)/shard_map/pallas_call | solution.py:481
  71.1 1.5 %copy.16 = bf16[16,2048]{1,0:T(8,128)(2,1)} copy(bf16[16,2048]{1,0:T(8,128)(2,1)} %get-tuple-element.12) | data formatting | bytes 131072
  72.6 1.5 %copy.17 = bf16[16,2048]{1,0:T(8,128)(2,1)} copy(bf16[16,2048]{1,0:T(8,128)(2,1)} %get-tuple-element.13) | data formatting | bytes 131072
  74.0 1.3 %copy.18 = f32[16,8]{0,1:T(8,128)} copy(f32[16,8]{0,1:T(8,128)} %bitcast.5) | data formatting | bytes 1024

commit v3 on v2

--- a/solution.py
+++ b/solution.py
@@ -17,7 +17,6 @@
 TILE = 256
 CHUNK = 32
 LANES = 128
-RING_BIT = 3
 MESH = pl.DeviceIdType.MESH
 
 ORDER = [[(q + s) % 4 for s in range(4)] for q in range(PARTS)]
@@ -109,7 +108,6 @@
     width = tokens.shape[1]
     part = width // PARTS
     hidden = down.shape[2]
-    replicas = 1 << levels
     dp = lax.axis_index("dp")
     me = lax.axis_index("expert")
     mx, my = lax.div(me, 4), lax.rem(me, 4)
@@ -117,18 +115,11 @@
     def member(j):
         return (dp, flip(mx, j >> 2) * 4 + flip(my, j & 3))
 
-    def moved(step):
-        return (lax.rem(dp + step + replicas, replicas), me)
+    def bit(b):
+        return lax.rem(lax.div(dp, 1 << b), 2)
 
     def partner(b):
-        step = 1 << b
-        return (dp + step * (1 - 2 * lax.rem(lax.div(dp, step), 2)), me)
-
-    direct = min(levels, RING_BIT)
-    jump = 1 << RING_BIT
-    far = (replicas // jump) // 2
-    back_far = far // 2
-    ways = [1] * (far > 0) + [-1] * (back_far > 0)
+        return (dp + (1 << b) * (1 - 2 * bit(b)), me)
 
     tiny = [
         pltpu.make_async_copy(routes, routes_v, tiny_sem.at[0]),
@@ -139,13 +130,15 @@
     for copy in tiny:
         copy.start()
     barrier = pltpu.get_barrier_semaphore()
-    everyone = [member(j) for j in range(1, MEMBERS)] + [partner(b) for b in range(direct)]
-    if far > 1:
-        everyone += [moved(jump), moved(-jump)]
-    elif far:
-        everyone += [moved(jump)]
-    for other in everyone:
-        pl.semaphore_signal(barrier, inc=1, device_id=other, device_id_type=MESH)
+    for j in range(1, MEMBERS):
+        pl.semaphore_signal(barrier, inc=1, device_id=member(j), device_id_type=MESH)
+    heard = MEMBERS - 1
+    for b in range(levels):
+        heard = heard + bit(b)
+
+        @pl.when(bit(b) == 0)
+        def _():
+            pl.semaphore_signal(barrier, inc=1, device_id=partner(b), device_id_type=MESH)
 
     sources = (tokens, grads)
     local = []
@@ -188,7 +181,7 @@
     for j in range(MEMBERS):
         gsend[j] = gmat[j : j + 1, :]
 
-    pl.semaphore_wait(barrier, len(everyone))
+    pl.semaphore_wait(barrier, heard)
 
     def gather(a, q, s):
         n = a * PARTS + q
@@ -217,25 +210,7 @@
         )
 
     gates_to = [small(gsend, grecv, g_send, g_recv, j, j, member(j)) for j in range(1, MEMBERS)]
-    direct_to = [small(dsend, drecv, d_send, d_recv, 0, b, partner(b)) for b in range(direct)]
-
-    def ring_slot(way, d):
-        return direct + d - 1 + (far if way < 0 else 0)
-
-    def ring_hop(way, d):
-        src, index = (dsend, 0) if d == 1 else (drecv, ring_slot(way, d - 1))
-        return small(src, drecv, d_send, d_recv, index, ring_slot(way, d), moved(way * jump))
-
-    hops = {(1, d): ring_hop(1, d) for d in range(1, far + 1)}
-    hops.update({(-1, d): ring_hop(-1, d) for d in range(1, back_far + 1)})
-
-    def ring_round(d):
-        for way in ways:
-            if (way, d) in hops:
-                if d > 1:
-                    hops[way, d - 1].wait_recv()
-                hops[way, d].start()
-
+    spare_to = [small(dsend, drecv, d_send, d_recv, 0, b, partner(b)) for b in range(levels)]
     quot_to = [small(qsend, qrecv, q_send, q_recv, j, j, member(j)) for j in range(1, MEMBERS)]
 
     def step_on(a, s):
@@ -243,16 +218,11 @@
             gather(a, q, s - 1).wait_recv()
             gather(a, q, s).start()
 
-    for q in range(PARTS):
-        gather(0, q, 0).start()
     for copy in gates_to:
         copy.start()
-    for q in range(PARTS):
-        gather(1, q, 0).start()
-    for copy in local:
-        copy.wait()
-    step_on(0, 1)
-    step_on(1, 1)
+    for a in range(2):
+        for q in range(PARTS):
+            gather(a, q, 0).start()
 
     gmat[0:1, :] = gsend[0]
     for j in range(1, MEMBERS):
@@ -265,12 +235,17 @@
     cap = jnp.broadcast_to(cap_s[...].astype(jnp.float32), (1, LANES))
     taken = jnp.minimum(cap - jnp.minimum(load, cap), float(OVF))
     dsend[0] = taken[0:1, :]
-    ring_round(1)
-    for copy in direct_to:
-        copy.start()
-
-    step_on(0, 2)
-    step_on(1, 2)
+    for b in range(levels):
+
+        @pl.when(bit(b) == 1)
+        def _():
+            spare_to[b].start()
+
+    for copy in local:
+        copy.wait()
+    for s in range(1, 4):
+        step_on(0, s)
+        step_on(1, s)
     big0 = lax.broadcasted_iota(jnp.int32, (LANES, LANES), 0)
     big1 = lax.broadcasted_iota(jnp.int32, (LANES, LANES), 1)
     ahead = jnp.where(big0 < big1, 1.0, 0.0).astype(jnp.bfloat16)
@@ -279,12 +254,6 @@
     col_home = recode(lax.broadcasted_iota(jnp.int32, (MEMBERS, MEMBERS), 1) ^ my_code)
     earlier = jnp.where(col_home < row_home, 1.0, 0.0).astype(jnp.bfloat16)
     position = within + nn_dot(earlier, counts)
-    ring_round(2)
-    step_on(0, 3)
-    ring_round(3)
-    step_on(1, 3)
-    ring_round(4)
-
     for q in range(PARTS):
         gather(0, q, 3).wait_recv()
     for copy in weights[:4]:
@@ -327,27 +296,6 @@
 
     lax.fori_loop(0, hidden // TILE, forward_tile, 0)
 
-    limit = jnp.zeros((1, LANES), jnp.float32) + cap
-    for b in range(direct):
-        direct_to[b].wait_recv()
-        limit += drecv[b] * (mask_s[...] == 1 << b).astype(jnp.float32)
-    for way, d in hops:
-        if (way, d + 1) not in hops:
-            hops[way, d].wait_recv()
-    for b in range(direct, levels):
-        d = 1 << (b - direct)
-        wanted = (mask_s[...] == 1 << b).astype(jnp.float32)
-        behind = drecv[ring_slot(1, d)]
-        if d < far:
-            upper = lax.rem(lax.div(dp, 1 << b), 2).astype(jnp.float32)
-            behind = upper * behind + (1.0 - upper) * drecv[ring_slot(-1, d)]
-        limit += wanted * behind
-    gkeep[...] = jnp.where(position < limit, mat, 0.0)
-    for j in range(MEMBERS):
-        row = jnp.broadcast_to(gkeep[j : j + 1, :], (TOK, LANES))
-        column = jnp.sum(jnp.where(lane == sub, row, 0.0), axis=1, keepdims=True)
-        gcol[j * TOK : (j + 1) * TOK, :] = jnp.broadcast_to(column, (TOK, LANES))
-
     def reduce(a, q, r):
         n = a * PARTS + q
         rows = slice(STEP_AT[r], STEP_AT[r] + STEP_ROWS[r])
@@ -368,21 +316,16 @@
     def produce(a, q, ref, weight):
         n = a * PARTS + q
         tile = min(TILE, part)
-        gate = permuted(gcol, q)
-        gate = jnp.concatenate([gate] * (tile // LANES), axis=1)
         for c in range(part // tile):
             cols = slice(c * tile, (c + 1) * tile)
             rows = slice(q * part + c * tile, q * part + (c + 1) * tile)
-            value = nt_dot(permuted(ref, q), weight[rows, :]) * gate
-            sb[n, 0:HALF, cols] = value[HALF:, :].astype(jnp.bfloat16)
-            acc[n, :, cols] = value[:HALF, :]
-        reduce(a, q, 0).start()
+            acc[n, :, cols] = nt_dot(permuted(ref, q), weight[rows, :])
 
     def pass_on(a, q, r):
         n = a * PARTS + q
         reduce(a, q, r - 1).wait_recv()
         size = STEP_ROWS[r]
-        total = acc[n, size : 2 * size, :]
+        total = acc[n, size : 2 * size, :] * gate_rows(q, size // TOK, size // TOK)
         for i in range(r):
             at = STEP_AT[i] + size
             total += rb[n, at : at + size, :].astype(jnp.float32)
@@ -392,7 +335,7 @@
     def finish(a, q, ref):
         n = a * PARTS + q
         reduce(a, q, 3).wait_recv()
-        total = acc[n, 0:TOK, :]
+        total = acc[n, 0:TOK, :] * gate_rows(q, 0, 1)
         for i in range(4):
             total += rb[n, STEP_AT[i] : STEP_AT[i] + TOK, :].astype(jnp.float32)
         ref[:, q * part : (q + 1) * part] = total.astype(jnp.bfloat16)
@@ -431,6 +374,41 @@
     for q in range(PARTS):
         produce(1, q, dpre, gu_v)
 
+    for b in range(levels):
+
+        @pl.when(bit(b) == 0)
+        def _():
+            spare_to[b].wait_recv()
+            spare_to[b].start()
+
+    for b in range(levels):
+
+        @pl.when(bit(b) == 1)
+        def _():
+            spare_to[b].wait_recv()
+
+    limit = cap
+    for b in range(levels):
+        limit += drecv[b] * (mask_s[...] == 1 << b).astype(jnp.float32)
+    gkeep[...] = jnp.where(position < limit, mat, 0.0)
+    for j in range(MEMBERS):
+        row = jnp.broadcast_to(gkeep[j : j + 1, :], (TOK, LANES))
+        column = jnp.sum(jnp.where(lane == sub, row, 0.0), axis=1, keepdims=True)
+        gcol[j * TOK : (j + 1) * TOK, :] = jnp.broadcast_to(column, (TOK, LANES))
+
+    def gate_rows(q, first, count):
+        rows = [gcol[SLOT[q][p] * TOK : (SLOT[q][p] + 1) * TOK, :] for p in range(first, first + count)]
+        return jnp.concatenate([jnp.concatenate(rows, axis=0)] * (part // LANES), axis=1)
+
+    for a in range(2):
+        for q in range(PARTS):
+            n = a * PARTS + q
+            for p in range(MEMBERS // 2, MEMBERS):
+                rows = slice(p * TOK, (p + 1) * TOK)
+                scaled = acc[n, rows, :] * gate_rows(q, p, 1)
+                sb[n, p * TOK - HALF : (p + 1) * TOK - HALF, :] = scaled.astype(jnp.bfloat16)
+            reduce(a, q, 0).start()
+
     for j in range(MEMBERS):
         column = jnp.sum(ggacc[j * TOK : (j + 1) * TOK, :], axis=1, keepdims=True)
         row = jnp.sum(jnp.where(lane == sub, column, 0.0), axis=0, keepdims=True)
@@ -464,7 +442,7 @@
             for s in range(4):
                 gather(a, q, s).wait_send()
                 reduce(a, q, s).wait_send()
-    for copy in gates_to + direct_to + list(hops.values()) + quot_to:
+    for copy in gates_to + spare_to + quot_to:
         copy.wait_send()
 
 
@@ -493,7 +471,7 @@
             pltpu.VMEM((streams, ROWS, part), b16),
             pltpu.VMEM((streams, 240, part), b16),
             pltpu.VMEM((streams, 240, part), b16),
-            pltpu.VMEM((streams, HALF, part), f32),
+            pltpu.VMEM((streams, ROWS, part), f32),
             pltpu.VMEM((ROWS, hidden), f32),
             pltpu.VMEM((ROWS, hidden), f32),
             pltpu.VMEM((ROWS, hidden), b16),

time: 75.6 us -> 71.1 us (0.940)
  the two profiles are of different devices: /device:TPU:8 before, /device:TPU:992 now
where the time goes in v3:
time: 71.1 us; the launch traced here: 70.8 us
  Pallas kernels  64.7 us (91%)
  local copies, waits for them, and re-layouts  4.22 us (6%)
  between operations  1.93 us (3%)
    pallas_call x1, Pallas kernels, body(): pl.pallas_call(functools.partial(kernel, levels), out_shape=(jax.ShapeDty...  64.7 us
    unnamed x3, local copies, waits for them, and re-layouts  4.22 us

profile of v3, /device:TPU:992, one launch (start us, length us, event | category | flops | bytes accessed | tf_op | source)
XLA Modules:
  0.0 70.8 jit_solution(255624748835099964)
XLA Ops:
  1.9 64.7 %shard_map.103 = (bf16[16,2048]{1,0:T(8,128)(2,1)}, bf16[16,2048]{1,0:T(8,128)(2,1)}, f32[8,16]{1,0:T(8,128)}) custom-call(bf16[16,2048]{1,0:T(8,128)(2,1)} %tokens.1, bf16[16,2048]{1,0:T(8,128)(2,1)} %grads.1, bf16[8,16]{1,0:T(8,128)(2,1)} %bitcast.7, s32[8,16]{1,0:T(8,128)} %bitcast.6, s32[1,1]{1,0:T(1,128)S(6)} %copy.14.capacity, ...), custom_call_target="tpu_custom_call" | custom-call | flops 4831838208 | bytes 9437184 | tf_op jit(solution)/shard_map/pallas_call | solution.py:459
  66.6 1.5 %copy.16 = bf16[16,2048]{1,0:T(8,128)(2,1)} copy(bf16[16,2048]{1,0:T(8,128)(2,1)} %get-tuple-element.12) | data formatting | bytes 131072
  68.1 1.5 %copy.17 = bf16[16,2048]{1,0:T(8,128)(2,1)} copy(bf16[16,2048]{1,0:T(8,128)(2,1)} %get-tuple-element.13) | data formatting | bytes 131072
  69.5 1.3 %copy.18 = f32[16,8]{0,1:T(8,128)} copy(f32[16,8]{0,1:T(8,128)} %bitcast.5) | data formatting | bytes 1024

commit v4 on v3

--- a/solution.py
+++ b/solution.py
@@ -85,7 +85,9 @@
     grecv,
     gmat,
     gkeep,
+    knear,
     gcol,
+    gnear,
     ggacc,
     qsend,
     qrecv,
@@ -104,6 +106,9 @@
     q_recv,
     d_send,
     d_recv,
+    k_send,
+    k_recv,
+    ready,
 ):
     width = tokens.shape[1]
     part = width // PARTS
@@ -182,6 +187,12 @@
         gsend[j] = gmat[j : j + 1, :]
 
     pl.semaphore_wait(barrier, heard)
+    for b in range(levels):
+
+        @pl.when(bit(b) == 1)
+        def _():
+            pl.semaphore_signal(ready.at[b], inc=1, device_id=partner(b), device_id_type=MESH)
+
 
     def gather(a, q, s):
         n = a * PARTS + q
@@ -223,6 +234,10 @@
     for a in range(2):
         for q in range(PARTS):
             gather(a, q, 0).start()
+    for copy in local:
+        copy.wait()
+    step_on(0, 1)
+    step_on(1, 1)
 
     gmat[0:1, :] = gsend[0]
     for j in range(1, MEMBERS):
@@ -241,9 +256,7 @@
         def _():
             spare_to[b].start()
 
-    for copy in local:
-        copy.wait()
-    for s in range(1, 4):
+    for s in range(2, 4):
         step_on(0, s)
         step_on(1, s)
     big0 = lax.broadcasted_iota(jnp.int32, (LANES, LANES), 0)
@@ -319,26 +332,10 @@
         for c in range(part // tile):
             cols = slice(c * tile, (c + 1) * tile)
             rows = slice(q * part + c * tile, q * part + (c + 1) * tile)
-            acc[n, :, cols] = nt_dot(permuted(ref, q), weight[rows, :])
-
-    def pass_on(a, q, r):
-        n = a * PARTS + q
-        reduce(a, q, r - 1).wait_recv()
-        size = STEP_ROWS[r]
-        total = acc[n, size : 2 * size, :] * gate_rows(q, size // TOK, size // TOK)
-        for i in range(r):
-            at = STEP_AT[i] + size
-            total += rb[n, at : at + size, :].astype(jnp.float32)
-        sb[n, STEP_AT[r] : STEP_AT[r] + size, :] = total.astype(jnp.bfloat16)
-        reduce(a, q, r).start()
-
-    def finish(a, q, ref):
-        n = a * PARTS + q
-        reduce(a, q, 3).wait_recv()
-        total = acc[n, 0:TOK, :] * gate_rows(q, 0, 1)
-        for i in range(4):
-            total += rb[n, STEP_AT[i] : STEP_AT[i] + TOK, :].astype(jnp.float32)
-        ref[:, q * part : (q + 1) * part] = total.astype(jnp.bfloat16)
+            value = nt_dot(permuted(ref, q), weight[rows, :])
+            sb[n, 0:HALF, cols] = value[HALF:, :].astype(jnp.bfloat16)
+            acc[n, :, cols] = value[:HALF, :]
+        reduce(a, q, 0).start()
 
     for copy in weights[4:]:
         copy.wait()
@@ -378,36 +375,79 @@
 
         @pl.when(bit(b) == 0)
         def _():
-            spare_to[b].wait_recv()
+            pl.semaphore_wait(ready.at[b], 1)
             spare_to[b].start()
-
-    for b in range(levels):
-
-        @pl.when(bit(b) == 1)
-        def _():
-            spare_to[b].wait_recv()
 
     limit = cap
     for b in range(levels):
+        spare_to[b].wait_recv()
         limit += drecv[b] * (mask_s[...] == 1 << b).astype(jnp.float32)
     gkeep[...] = jnp.where(position < limit, mat, 0.0)
+    near_to = [
+        pltpu.make_async_remote_copy(
+            src_ref=gkeep,
+            dst_ref=knear.at[i],
+            send_sem=k_send.at[i],
+            recv_sem=k_recv.at[i],
+            device_id=member(1 << i),
+            device_id_type=MESH,
+        )
+        for i in range(4)
+    ]
+    for copy in near_to:
+        copy.start()
+
+    def spread(row):
+        row = jnp.broadcast_to(row, (TOK, LANES))
+        column = jnp.sum(jnp.where(lane == sub, row, 0.0), axis=1, keepdims=True)
+        return jnp.broadcast_to(column, (TOK, LANES))
+
     for j in range(MEMBERS):
-        row = jnp.broadcast_to(gkeep[j : j + 1, :], (TOK, LANES))
-        column = jnp.sum(jnp.where(lane == sub, row, 0.0), axis=1, keepdims=True)
-        gcol[j * TOK : (j + 1) * TOK, :] = jnp.broadcast_to(column, (TOK, LANES))
+        gcol[j * TOK : (j + 1) * TOK, :] = spread(gkeep[j : j + 1, :])
+    for i in range(4):
+        near_to[i].wait_recv()
+        for j in range(MEMBERS):
+            if not j >> i & 1:
+                other = j ^ (1 << i)
+                gnear[i, j * TOK : (j + 1) * TOK, :] = spread(knear[i, other : other + 1, :])
+
+    def widen(rows):
+        return jnp.concatenate([jnp.concatenate(rows, axis=0)] * (part // LANES), axis=1)
 
     def gate_rows(q, first, count):
-        rows = [gcol[SLOT[q][p] * TOK : (SLOT[q][p] + 1) * TOK, :] for p in range(first, first + count)]
-        return jnp.concatenate([jnp.concatenate(rows, axis=0)] * (part // LANES), axis=1)
-
-    for a in range(2):
-        for q in range(PARTS):
-            n = a * PARTS + q
-            for p in range(MEMBERS // 2, MEMBERS):
-                rows = slice(p * TOK, (p + 1) * TOK)
-                scaled = acc[n, rows, :] * gate_rows(q, p, 1)
-                sb[n, p * TOK - HALF : (p + 1) * TOK - HALF, :] = scaled.astype(jnp.bfloat16)
-            reduce(a, q, 0).start()
+        slots_in = [SLOT[q][p] * TOK for p in range(first, first + count)]
+        return widen([gcol[at : at + TOK, :] for at in slots_in])
+
+    def near_rows(q, first, count):
+        slots_in = [SLOT[q][p] * TOK for p in range(first, first + count)]
+        return widen([gnear[ORDER[q][3], at : at + TOK, :] for at in slots_in])
+
+    def total_of(n, q, first, count, steps):
+        size = count * TOK
+        at = first * TOK
+        total = acc[n, at : at + size, :] * gate_rows(q, first, count)
+        for i in range(steps):
+            term = rb[n, STEP_AT[i] + at : STEP_AT[i] + at + size, :].astype(jnp.float32)
+            total += term * near_rows(q, first, count) if i == 0 else term
+        return total.astype(jnp.bfloat16)
+
+    def pass_on(a, q, r):
+        n = a * PARTS + q
+        reduce(a, q, r - 1).wait_recv()
+        size = STEP_ROWS[r]
+        count = size // TOK
+        sb[n, STEP_AT[r] : STEP_AT[r] + size, :] = total_of(n, q, count, count, r)
+        reduce(a, q, r).start()
+
+    def finish(a, q, ref):
+        n = a * PARTS + q
+        reduce(a, q, 3).wait_recv()
+        ref[:, q * part : (q + 1) * part] = total_of(n, q, 0, 1, 4)
+
+    for q in range(PARTS):
+        pass_on(0, q, 1)
+    for q in range(PARTS):
+        pass_on(1, q, 1)
 
     for j in range(MEMBERS):
         column = jnp.sum(ggacc[j * TOK : (j + 1) * TOK, :], axis=1, keepdims=True)
@@ -416,7 +456,7 @@
     for copy in quot_to:
         copy.start()
 
-    for r in range(1, 4):
+    for r in range(2, 4):
         for q in range(PARTS):
             pass_on(0, q, r)
         for q in range(PARTS):
@@ -442,7 +482,7 @@
             for s in range(4):
                 gather(a, q, s).wait_send()
                 reduce(a, q, s).wait_send()
-    for copy in gates_to + spare_to + quot_to:
+    for copy in gates_to + spare_to + quot_to + near_to:
         copy.wait_send()
 
 
@@ -471,7 +511,7 @@
             pltpu.VMEM((streams, ROWS, part), b16),
             pltpu.VMEM((streams, 240, part), b16),
             pltpu.VMEM((streams, 240, part), b16),
-            pltpu.VMEM((streams, ROWS, part), f32),
+            pltpu.VMEM((streams, HALF, part), f32),
             pltpu.VMEM((ROWS, hidden), f32),
             pltpu.VMEM((ROWS, hidden), f32),
             pltpu.VMEM((ROWS, hidden), b16),
@@ -486,7 +526,9 @@
             pltpu.VMEM((MEMBERS, 1, LANES), f32),
             pltpu.VMEM((MEMBERS, LANES), f32),
             pltpu.VMEM((MEMBERS, LANES), f32),
+            pltpu.VMEM((4, MEMBERS, LANES), f32),
             pltpu.VMEM((ROWS, LANES), f32),
+            pltpu.VMEM((4, ROWS, LANES), f32),
             pltpu.VMEM((ROWS, LANES), f32),
             pltpu.VMEM((MEMBERS, 1, LANES), f32),
             pltpu.VMEM((MEMBERS, 1, LANES), f32),
@@ -505,6 +547,9 @@
             dma((MEMBERS,)),
             dma((16,)),
             dma((16,)),
+            dma((4,)),
+            dma((4,)),
+            pltpu.SemaphoreType.REGULAR((max(levels, 1),)),
         ],
         compiler_params=pltpu.CompilerParams(
             collective_id=0, has_side_effects=True, vmem_limit_bytes=60 * 1024 * 1024

time: 71.1 us -> 67.4 us (0.948)
  Pallas kernels: 64.7 us -> 60.9 us
    pallas_call x1, Pallas kernels: 64.7 us -> 60.9 us  [body(): pl.pallas_call(functools.partial(kernel, levels), out_shape=(jax.ShapeDty...]
where the time goes in v4:
time: 67.4 us; the launch traced here: 67.1 us
  Pallas kernels  60.9 us (90%)
  local copies, waits for them, and re-layouts  4.22 us (6%)
  between operations  1.93 us (3%)
    pallas_call x1, Pallas kernels, body(): pl.pallas_call(functools.partial(kernel, levels), out_shape=(jax.ShapeDty...  60.9 us
    unnamed x3, local copies, waits for them, and re-layouts  4.22 us

profile of v4, /device:TPU:992, one launch (start us, length us, event | category | flops | bytes accessed | tf_op | source)
XLA Modules:
  0.0 67.1 jit_solution(16816139174689214467)
XLA Ops:
  1.9 60.9 %shard_map.103 = (bf16[16,2048]{1,0:T(8,128)(2,1)}, bf16[16,2048]{1,0:T(8,128)(2,1)}, f32[8,16]{1,0:T(8,128)}) custom-call(bf16[16,2048]{1,0:T(8,128)(2,1)} %tokens.1, bf16[16,2048]{1,0:T(8,128)(2,1)} %grads.1, bf16[8,16]{1,0:T(8,128)(2,1)} %bitcast.7, s32[8,16]{1,0:T(8,128)} %bitcast.6, s32[1,1]{1,0:T(1,128)S(6)} %copy.14.capacity, ...), custom_call_target="tpu_custom_call" | custom-call | flops 4831838208 | bytes 9437184 | tf_op jit(solution)/shard_map/pallas_call | solution.py:499
  62.9 1.5 %copy.16 = bf16[16,2048]{1,0:T(8,128)(2,1)} copy(bf16[16,2048]{1,0:T(8,128)(2,1)} %get-tuple-element.12) | data formatting | bytes 131072
  64.3 1.5 %copy.17 = bf16[16,2048]{1,0:T(8,128)(2,1)} copy(bf16[16,2048]{1,0:T(8,128)(2,1)} %get-tuple-element.13) | data formatting | bytes 131072
  65.8 1.3 %copy.18 = f32[16,8]{0,1:T(8,128)} copy(f32[16,8]{0,1:T(8,128)} %bitcast.5) | data formatting | bytes 1024

commit v5 on v4

--- a/solution.py
+++ b/solution.py
@@ -85,9 +85,15 @@
     grecv,
     gmat,
     gkeep,
+    gpos,
     knear,
     gcol,
     gnear,
+    pcol,
+    pnear,
+    lsend,
+    lnear,
+    qrow,
     ggacc,
     qsend,
     qrecv,
@@ -108,6 +114,8 @@
     d_recv,
     k_send,
     k_recv,
+    l_send,
+    l_recv,
     ready,
 ):
     width = tokens.shape[1]
@@ -220,6 +228,16 @@
             device_id_type=MESH,
         )
 
+    def near(src, dst, send, recv, i):
+        return pltpu.make_async_remote_copy(
+            src_ref=src,
+            dst_ref=dst,
+            send_sem=send.at[i],
+            recv_sem=recv.at[i],
+            device_id=member(1 << i),
+            device_id_type=MESH,
+        )
+
     gates_to = [small(gsend, grecv, g_send, g_recv, j, j, member(j)) for j in range(1, MEMBERS)]
     spare_to = [small(dsend, drecv, d_send, d_recv, 0, b, partner(b)) for b in range(levels)]
     quot_to = [small(qsend, qrecv, q_send, q_recv, j, j, member(j)) for j in range(1, MEMBERS)]
@@ -267,6 +285,11 @@
     col_home = recode(lax.broadcasted_iota(jnp.int32, (MEMBERS, MEMBERS), 1) ^ my_code)
     earlier = jnp.where(col_home < row_home, 1.0, 0.0).astype(jnp.bfloat16)
     position = within + nn_dot(earlier, counts)
+    gpos[0:MEMBERS, :] = mat
+    gpos[MEMBERS : 2 * MEMBERS, :] = position
+    near_to = [near(gpos, knear.at[i], k_send, k_recv, i) for i in range(4)]
+    for copy in near_to:
+        copy.start()
     for q in range(PARTS):
         gather(0, q, 3).wait_recv()
     for copy in weights[:4]:
@@ -371,6 +394,29 @@
     for q in range(PARTS):
         produce(1, q, dpre, gu_v)
 
+    def spread(row):
+        row = jnp.broadcast_to(row, (TOK, LANES))
+        column = jnp.sum(jnp.where(lane == sub, row, 0.0), axis=1, keepdims=True)
+        return jnp.broadcast_to(column, (TOK, LANES))
+
+    for j in range(MEMBERS):
+        rows = slice(j * TOK, (j + 1) * TOK)
+        gcol[rows, :] = spread(gpos[j : j + 1, :])
+        pcol[rows, :] = spread(gpos[MEMBERS + j : MEMBERS + j + 1, :])
+        column = jnp.sum(ggacc[rows, :], axis=1, keepdims=True)
+        qrow[j : j + 1, :] = jnp.sum(jnp.where(lane == sub, column, 0.0), axis=0, keepdims=True)
+    for i in range(4):
+        near_to[i].wait_recv()
+        for j in range(MEMBERS):
+            rows = slice(j * TOK, (j + 1) * TOK)
+            other = j ^ (1 << i)
+            if j >> i & 1:
+                gnear[i, rows, :] = jnp.zeros((TOK, LANES), jnp.float32)
+                pnear[i, rows, :] = jnp.zeros((TOK, LANES), jnp.float32)
+            else:
+                gnear[i, rows, :] = spread(knear[i, other : other + 1, :])
+                pnear[i, rows, :] = spread(knear[i, MEMBERS + other : MEMBERS + other + 1, :])
+
     for b in range(levels):
 
         @pl.when(bit(b) == 0)
@@ -382,34 +428,20 @@
     for b in range(levels):
         spare_to[b].wait_recv()
         limit += drecv[b] * (mask_s[...] == 1 << b).astype(jnp.float32)
-    gkeep[...] = jnp.where(position < limit, mat, 0.0)
-    near_to = [
-        pltpu.make_async_remote_copy(
-            src_ref=gkeep,
-            dst_ref=knear.at[i],
-            send_sem=k_send.at[i],
-            recv_sem=k_recv.at[i],
-            device_id=member(1 << i),
-            device_id_type=MESH,
-        )
-        for i in range(4)
-    ]
-    for copy in near_to:
+    lsend[0] = limit
+    limits_to = [near(lsend.at[0], lnear.at[i], l_send, l_recv, i) for i in range(4)]
+    for copy in limits_to:
         copy.start()
-
-    def spread(row):
-        row = jnp.broadcast_to(row, (TOK, LANES))
-        column = jnp.sum(jnp.where(lane == sub, row, 0.0), axis=1, keepdims=True)
-        return jnp.broadcast_to(column, (TOK, LANES))
-
+    gcol[...] = jnp.where(pcol[...] < limit, gcol[...], 0.0)
+    kept = (mat > 0.0) & (position < limit)
+    gkeep[...] = jnp.where(kept, qrow[...], 0.0)
     for j in range(MEMBERS):
-        gcol[j * TOK : (j + 1) * TOK, :] = spread(gkeep[j : j + 1, :])
+        qsend[j] = gkeep[j : j + 1, :]
+    for copy in quot_to:
+        copy.start()
     for i in range(4):
-        near_to[i].wait_recv()
-        for j in range(MEMBERS):
-            if not j >> i & 1:
-                other = j ^ (1 << i)
-                gnear[i, j * TOK : (j + 1) * TOK, :] = spread(knear[i, other : other + 1, :])
+        limits_to[i].wait_recv()
+        gnear[i] = jnp.where(pnear[i] < lnear[i], gnear[i], 0.0)
 
     def widen(rows):
         return jnp.concatenate([jnp.concatenate(rows, axis=0)] * (part // LANES), axis=1)
@@ -449,13 +481,6 @@
     for q in range(PARTS):
         pass_on(1, q, 1)
 
-    for j in range(MEMBERS):
-        column = jnp.sum(ggacc[j * TOK : (j + 1) * TOK, :], axis=1, keepdims=True)
-        row = jnp.sum(jnp.where(lane == sub, column, 0.0), axis=0, keepdims=True)
-        qsend[j] = jnp.where(gkeep[j : j + 1, :] > 0.0, row, 0.0)
-    for copy in quot_to:
-        copy.start()
-
     for r in range(2, 4):
         for q in range(PARTS):
             pass_on(0, q, r)
@@ -482,7 +507,7 @@
             for s in range(4):
                 gather(a, q, s).wait_send()
                 reduce(a, q, s).wait_send()
-    for copy in gates_to + spare_to + quot_to + near_to:
+    for copy in gates_to + spare_to + quot_to + near_to + limits_to:
         copy.wait_send()
 
 
@@ -526,9 +551,15 @@
             pltpu.VMEM((MEMBERS, 1, LANES), f32),
             pltpu.VMEM((MEMBERS, LANES), f32),
             pltpu.VMEM((MEMBERS, LANES), f32),
-            pltpu.VMEM((4, MEMBERS, LANES), f32),
+            pltpu.VMEM((2 * MEMBERS, LANES), f32),
+            pltpu.VMEM((4, 2 * MEMBERS, LANES), f32),
             pltpu.VMEM((ROWS, LANES), f32),
             pltpu.VMEM((4, ROWS, LANES), f32),
+            pltpu.VMEM((ROWS, LANES), f32),
+            pltpu.VMEM((4, ROWS, LANES), f32),
+            pltpu.VMEM((1, 1, LANES), f32),
+            pltpu.VMEM((4, 1, LANES), f32),
+            pltpu.VMEM((MEMBERS, LANES), f32),
             pltpu.VMEM((ROWS, LANES), f32),
             pltpu.VMEM((MEMBERS, 1, LANES), f32),
             pltpu.VMEM((MEMBERS, 1, LANES), f32),
@@ -547,6 +578,8 @@
             dma((MEMBERS,)),
             dma((16,)),
             dma((16,)),
+            dma((4,)),
+            dma((4,)),
             dma((4,)),
             dma((4,)),
             pltpu.SemaphoreType.REGULAR((max(levels, 1),)),

time: 67.4 us -> 68 us (level)
  Pallas kernels: 60.9 us -> 61.6 us
where the time goes in v5:
time: 68 us; the launch traced here: 67.7 us
  Pallas kernels  61.6 us (91%)
  local copies, waits for them, and re-layouts  4.22 us (6%)
  between operations  1.93 us (3%)
    pallas_call x1, Pallas kernels, body(): pl.pallas_call(functools.partial(kernel, levels), out_shape=(jax.ShapeDty...  61.6 us
    unnamed x3, local copies, waits for them, and re-layouts  4.22 us

profile of v5, /device:TPU:992, one launch (start us, length us, event | category | flops | bytes accessed | tf_op | source)
XLA Modules:
  0.0 67.7 jit_solution(554839846018149945)
XLA Ops:
  1.9 61.6 %shard_map.103 = (bf16[16,2048]{1,0:T(8,128)(2,1)}, bf16[16,2048]{1,0:T(8,128)(2,1)}, f32[8,16]{1,0:T(8,128)}) custom-call(bf16[16,2048]{1,0:T(8,128)(2,1)} %tokens.1, bf16[16,2048]{1,0:T(8,128)(2,1)} %grads.1, bf16[8,16]{1,0:T(8,128)(2,1)} %bitcast.7, s32[8,16]{1,0:T(8,128)} %bitcast.6, s32[1,1]{1,0:T(1,128)S(6)} %copy.14.capacity, ...), custom_call_target="tpu_custom_call" | custom-call | flops 4831838208 | bytes 9437184 | tf_op jit(solution)/shard_map/pallas_call | solution.py:524
  63.5 1.5 %copy.16 = bf16[16,2048]{1,0:T(8,128)(2,1)} copy(bf16[16,2048]{1,0:T(8,128)(2,1)} %get-tuple-element.12) | data formatting | bytes 131072
  65.0 1.5 %copy.17 = bf16[16,2048]{1,0:T(8,128)(2,1)} copy(bf16[16,2048]{1,0:T(8,128)(2,1)} %get-tuple-element.13) | data formatting | bytes 131072
  66.5 1.3 %copy.18 = f32[16,8]{0,1:T(8,128)} copy(f32[16,8]{0,1:T(8,128)} %bitcast.5) | data formatting | bytes 1024

commit v6 on v5

--- a/solution.py
+++ b/solution.py
@@ -247,15 +247,16 @@
             gather(a, q, s - 1).wait_recv()
             gather(a, q, s).start()
 
+    for a in range(2):
+        for q in range(PARTS):
+            gather(a, q, 0).start()
     for copy in gates_to:
         copy.start()
-    for a in range(2):
-        for q in range(PARTS):
-            gather(a, q, 0).start()
     for copy in local:
         copy.wait()
-    step_on(0, 1)
-    step_on(1, 1)
+    for s in range(1, 3):
+        step_on(0, s)
+        step_on(1, s)
 
     gmat[0:1, :] = gsend[0]
     for j in range(1, MEMBERS):
@@ -274,9 +275,8 @@
         def _():
             spare_to[b].start()
 
-    for s in range(2, 4):
-        step_on(0, s)
-        step_on(1, s)
+    step_on(0, 3)
+    step_on(1, 3)
     big0 = lax.broadcasted_iota(jnp.int32, (LANES, LANES), 0)
     big1 = lax.broadcasted_iota(jnp.int32, (LANES, LANES), 1)
     ahead = jnp.where(big0 < big1, 1.0, 0.0).astype(jnp.bfloat16)

time: 68 us -> 68.1 us (level)
  no operation moved by 1% of the time
where the time goes in v6:
time: 68.1 us; the launch traced here: 67.8 us
  Pallas kernels  61.6 us (90%)
  local copies, waits for them, and re-layouts  4.22 us (6%)
  between operations  1.93 us (3%)
    pallas_call x1, Pallas kernels, body(): pl.pallas_call(functools.partial(kernel, levels), out_shape=(jax.ShapeDty...  61.6 us
    unnamed x3, local copies, waits for them, and re-layouts  4.22 us

profile of v6, /device:TPU:992, one launch (start us, length us, event | category | flops | bytes accessed | tf_op | source)
XLA Modules:
  0.0 67.8 jit_solution(10068598380148714349)
XLA Ops:
  1.9 61.6 %shard_map.103 = (bf16[16,2048]{1,0:T(8,128)(2,1)}, bf16[16,2048]{1,0:T(8,128)(2,1)}, f32[8,16]{1,0:T(8,128)}) custom-call(bf16[16,2048]{1,0:T(8,128)(2,1)} %tokens.1, bf16[16,2048]{1,0:T(8,128)(2,1)} %grads.1, bf16[8,16]{1,0:T(8,128)(2,1)} %bitcast.7, s32[8,16]{1,0:T(8,128)} %bitcast.6, s32[1,1]{1,0:T(1,128)S(6)} %copy.14.capacity, ...), custom_call_target="tpu_custom_call" | custom-call | flops 4831838208 | bytes 9437184 | tf_op jit(solution)/shard_map/pallas_call | solution.py:524
  63.5 1.5 %copy.16 = bf16[16,2048]{1,0:T(8,128)(2,1)} copy(bf16[16,2048]{1,0:T(8,128)(2,1)} %get-tuple-element.12) | data formatting | bytes 131072
  65.0 1.5 %copy.17 = bf16[16,2048]{1,0:T(8,128)(2,1)} copy(bf16[16,2048]{1,0:T(8,128)(2,1)} %get-tuple-element.13) | data formatting | bytes 131072
  66.5 1.3 %copy.18 = f32[16,8]{0,1:T(8,128)} copy(f32[16,8]{0,1:T(8,128)} %bitcast.5) | data formatting | bytes 1024
